TPU v7x, 128 devices: a whole 4x4x4 slice. The times are simulated.
128 devices in a mesh: pipe: 16 (over y, x), mp: 8 (over z, core).
Axes of the slice: x: 4, y: 4, z: 4, core: 2. Of those that a mesh axis runs over, the one named last changes fastest.
Arguments:
- context: bfloat16 [512, 4096], P('pipe', 'mp'), may hold values from -6 to 6
- residual_in: bfloat16 [512, 4608], P('pipe', 'mp'), may hold values from -6 to 6
- o_weight: bfloat16 [4096, 4608], P('mp', 'pipe'), may hold values from -0.09375 to 0.09375
- post_gain: float32 [4608], replicated, may hold values from 0.1 to 1.9
- final_gain: float32 [4608], replicated, may hold values from 0.1 to 1.9
- head_weight: bfloat16 [4608, 131072], P(None, ('pipe', 'mp')), may hold values from -0.26516504 to 0.26516504
- targets: int32 [512], replicated, may hold values from 0 to 131071
Outputs:
- mean_loss: float32 [], replicated
- head_grad: bfloat16 [4608, 131072], P(None, ('pipe', 'mp'))
- o_grad: bfloat16 [4096, 4608], P('mp', 'pipe')
- d_residual: bfloat16 [512, 4608], P('pipe', 'mp')
- d_context: bfloat16 [512, 4096], P('pipe', 'mp')
All inputs are finite; a program needn't handle non-finite values.
Results may differ from a plain program's by a relative error of at most 0.006.
Values may be sent and summed in bfloat16 or wider, within the bound.
A program may use at most 128 MiB of HBM per device.

v0:
```python
import jax
import jax.numpy as jnp
from jax import lax
from jax.sharding import PartitionSpec as P

epsilon = 1e-06
softcap = 30.0


def on_device(context, residual_in, o_weight, post_gain, final_gain, head_weight, targets):
    model_width = head_weight.shape[0]
    vocab_dev = head_weight.shape[1]
    share_cols = residual_in.shape[1]
    mp_index = lax.axis_index("mp")
    share_first = mp_index * share_cols
    vocab_first = (lax.axis_index("pipe") * lax.axis_size("mp") + mp_index) * vocab_dev
    o_full = lax.all_gather(o_weight, "pipe", axis=1, tiled=True)
    attn_part = jnp.dot(context, o_full, preferred_element_type=jnp.float32)
    post_share = lax.dynamic_slice_in_dim(post_gain, share_first, share_cols)
    final_share = lax.dynamic_slice_in_dim(final_gain, share_first, share_cols)
    attn_share = lax.psum_scatter(attn_part, "mp", scatter_dimension=1, tiled=True)
    attn_sq = lax.psum(jnp.sum(attn_share * attn_share, axis=-1, keepdims=True), "mp")
    inv_attn = lax.rsqrt(attn_sq / model_width + epsilon)
    stream = residual_in.astype(jnp.float32) + attn_share * inv_attn * post_share
    stream_sq = lax.psum(jnp.sum(stream * stream, axis=-1, keepdims=True), "mp")
    inv_stream = lax.rsqrt(stream_sq / model_width + epsilon)
    normed_share = (stream * inv_stream * final_share).astype(jnp.bfloat16)
    normed = lax.all_gather(normed_share, "mp", axis=1, tiled=True)
    all_rows = lax.all_gather(normed, "pipe", axis=0, tiled=True)
    logits = jnp.dot(all_rows, head_weight, preferred_element_type=jnp.float32)
    capped = softcap * jnp.tanh(logits / softcap)
    exp_logits = jnp.exp(capped)
    columns = vocab_first + lax.iota(jnp.int32, vocab_dev)
    target_hits = columns[None, :] == targets[:, None]
    part_total = jnp.sum(exp_logits, axis=-1)
    part_target = jnp.sum(jnp.where(target_hits, capped, jnp.float32(0.0)), axis=-1)
    totals, target_logit = lax.psum((part_total, part_target), ("pipe", "mp"))
    mean_loss = jnp.mean(jnp.log(totals) - target_logit)
    logit_grad = (exp_logits / totals[:, None] - target_hits.astype(jnp.float32)) * (
        1.0 - (capped / softcap) ** 2
    )
    logit_grad = logit_grad.astype(jnp.bfloat16)
    head_grad = jnp.dot(all_rows.T, logit_grad, preferred_element_type=jnp.float32).astype(
        jnp.bfloat16
    )
    grad_part = lax.psum_scatter(
        jnp.dot(logit_grad, head_weight.T, preferred_element_type=jnp.float32),
        "pipe",
        scatter_dimension=0,
        tiled=True,
    )
    grad_share = lax.psum_scatter(grad_part, "mp", scatter_dimension=1, tiled=True)
    upstream_grad = grad_share * final_share
    cross_sum = lax.psum(jnp.sum(stream * upstream_grad, axis=-1, keepdims=True), "mp")
    grad_stream = inv_stream * (upstream_grad - stream * inv_stream**2 * (cross_sum / model_width))
    scaled_grad = grad_stream * post_share
    cross_attn = lax.psum(jnp.sum(attn_share * scaled_grad, axis=-1, keepdims=True), "mp")
    attn_grad_share = inv_attn * (
        scaled_grad - attn_share * inv_attn**2 * (cross_attn / model_width)
    )
    grad_attn = lax.all_gather(attn_grad_share.astype(jnp.bfloat16), "mp", axis=1, tiled=True)
    d_residual = grad_stream.astype(jnp.bfloat16)
    d_context = jnp.dot(grad_attn, o_full.T, preferred_element_type=jnp.float32).astype(
        jnp.bfloat16
    )
    o_term = jnp.dot(context.T, grad_attn, preferred_element_type=jnp.float32)
    o_grad = lax.psum_scatter(o_term, "pipe", scatter_dimension=1, tiled=True).astype(jnp.bfloat16)
    return (mean_loss, head_grad, o_grad, d_residual, d_context)


def solution(mesh):
    placed = (
        P("pipe", "mp"),
        P("pipe", "mp"),
        P("mp", "pipe"),
        P(),
        P(),
        P(None, ("pipe", "mp")),
        P(),
    )
    return jax.shard_map(
        on_device,
        mesh=mesh,
        in_specs=placed,
        out_specs=(P(), P(None, ("pipe", "mp")), P("mp", "pipe"), P("pipe", "mp"), P("pipe", "mp")),
        check_vma=False,
    )
```

profile of v0, /device:TPU:1, one launch (start us, length us, event | category | flops | bytes accessed | tf_op | source)
XLA Modules:
  0.0 550.3 jit_solution(10140981614573931241)
XLA Ops:
  7.2 0.0 copy-start
  7.2 0.0 all-gather.5.cloned.1.call-start
  7.2 0.7 all-gather.5.cloned.1.call-update
  7.9 0.0 reduce-scatter.13.cloned.1.call-start
  8.0 59.3 %all-gather.5.cloned.1.call-done = bf16[512,4608]{0,1:T(8,128)(2,1)} async-done(((bf16[512,288]{0,1:T(8,128)(2,1)}), bf16[512,4608]{0,1:T(8,128)(2,1)}) %all-gather.5.cloned.1.call-update) | async-done | bytes 4718608 | tf_op jit(solution)/shard_map/all_gather | solution.py:17
  67.3 0.0 copy-done
  67.3 5.1 convolution_bitcast_fusion.1
  72.4 0.0 copy-start.1
  72.4 0.0 copy-start.2
  72.4 0.0 reduce-scatter.13.cloned.1.call-update
  72.4 0.0 all-gather.7.cloned.1.call-start
  72.5 0.8 dynamic_slice.6
  73.3 0.8 dynamic_slice.7
  74.0 29.5 %reduce-scatter.13.cloned.1.call-done = f32[576,32]{1,0:T(8,128)} async-done(((f32[4608,32]{1,0:T(8,128)}), f32[576,32]{1,0:T(8,128)}) %reduce-scatter.13.cloned.1.call-update) | async-done | bytes 73744
  103.5 1.1 copy.17
  104.6 0.1 multiply_reduce_fusion.3
  104.7 15.6 %psum.42 = f32[32,1]{0,1:T(1,128)S(1)} all-reduce(f32[32,1]{0,1:T(1,128)S(1)} %bitcast.52), channel_id=1, replica_groups=mesh['pipe'=16,'mp'=8] {'mp'}, use_global_device_ids=true, to_apply=%region_2.0 | all-reduce | flops 32 | bytes 256 | tf_op jit(solution)/shard_map/psum | solution.py:22
  120.3 0.0 copy-done.1
  120.3 0.2 multiply_reduce_fusion.2
  120.5 12.5 %psum.43 = f32[32,1]{0,1:T(1,128)S(1)} all-reduce(f32[32,1]{0,1:T(1,128)S(1)} %bitcast.53), channel_id=1, replica_groups=mesh['pipe'=16,'mp'=8] {'mp'}, use_global_device_ids=true, to_apply=%region_4.0 | all-reduce | flops 32 | bytes 256 | tf_op jit(solution)/shard_map/psum | solution.py:25
  133.1 0.1 fusion.4
  133.2 13.4 %all-gather = bf16[8,576,32]{1,2,0:T(8,128)(2,1)S(1)} all-gather(bf16[1,576,32]{1,2,0:T(8,128)(2,1)S(1)} %fusion.4), channel_id=1, replica_groups=mesh['pipe'=16,'mp'=8] {'mp'}, dimensions={0}, use_global_device_ids=true | all-gather | bytes 331776 | tf_op jit(solution)/shard_map/all_gather | solution.py:28
  146.6 0.1 copy.14
  146.7 1.0 reshape.19
  147.6 0.0 all-gather.7.cloned.1.call-update
  147.7 0.0 reduce-scatter.9.cloned.1.call-start
  147.7 53.1 %all-gather.7.cloned.1.call-done = bf16[512,4608]{1,0:T(8,128)(2,1)} async-done(((bf16[32,4608]{1,0:T(8,128)(2,1)}), bf16[512,4608]{1,0:T(8,128)(2,1)}) %all-gather.7.cloned.1.call-update) | async-done | bytes 4718608 | tf_op jit(solution)/shard_map/all_gather | solution.py:29
  200.8 0.0 copy-done.2
  200.8 9.6 %exponential_reduce_fusion = (f32[512]{0:T(512)S(1)}, f32[512]{0:T(512)S(1)}, f32[512,1024]{1,0:T(8,128)S(1)}) fusion(s32[512]{0:T(512)S(1)} %copy-done.2, s32[1024]{0:T(1024)S(1)} %iota_add_fusion, bf16[512,4608]{1,0:T(8,128)(2,1)} %all-gather.7.cloned.1.call-done, bf16[4608,1024]{1,0:T(8,128)(2,1)} %param.12), kind=kOutput, calls=%fused_computation.10 | convolution fusion | flops 4834982912 | bytes 16263168 | tf_op jit(solution)/shard_map/dot_general | solution.py:30
  210.4 64.8 %all-reduce = (f32[512]{0:T(512)S(1)}, f32[512]{0:T(512)S(1)}) all-reduce(f32[512]{0:T(512)S(1)} %get-tuple-element.6, f32[512]{0:T(512)S(1)} %get-tuple-element.5), channel_id=1, replica_groups=mesh['pipe'=16,'mp'=8] {'pipe','mp'}, use_global_device_ids=true, to_apply=%region_8.9 | all-reduce | flops 1024 | bytes 8192 | tf_op jit(solution)/shard_map/psum | solution.py:37
  275.2 11.9 %fusion.8 = f32[512,4608]{1,0:T(8,128)} fusion(bf16[4608,1024]{1,0:T(8,128)(2,1)} %param.12, f32[512,1024]{1,0:T(8,128)S(1)} %get-tuple-element.15, f32[512]{0:T(512)S(1)} %get-tuple-element.8, s32[1024]{0:T(1024)S(1)} %iota_add_fusion, s32[512]{0:T(512)S(1)} %copy-done.2), kind=kOutput, calls=%fused_computation.32 | convolution fusion | flops 4836556800 | bytes 20979712 | tf_op jit(solution)/shard_map/dot_general | solution.py:47
  287.1 0.0 reduce-scatter.9.cloned.1.call-update
  287.1 0.0 reduce-scatter.15.cloned.1.call-start
  287.2 83.5 %reduce-scatter.9.cloned.1.call-done = f32[32,4608]{1,0:T(8,128)} async-done(((f32[512,4608]{1,0:T(8,128)}), f32[32,4608]{1,0:T(8,128)}) %reduce-scatter.9.cloned.1.call-update) | async-done | bytes 589840 | tf_op jit(solution)/shard_map/reduce_scatter | solution.py:46
  370.7 3.1 copy.18
  373.9 0.0 reduce-scatter.15.cloned.1.call-update
  373.9 0.0 reduce-scatter.11.cloned.1.call-start
  374.0 31.6 %reduce-scatter.15.cloned.1.call-done = f32[576,32]{1,0:T(8,128)} async-done(((f32[4608,32]{1,0:T(8,128)}), f32[576,32]{1,0:T(8,128)}) %reduce-scatter.15.cloned.1.call-update) | async-done | bytes 73744
  405.5 1.1 copy.19
  406.6 0.2 multiply_reduce_fusion.1
  406.8 15.7 %psum.46 = f32[32,1]{0,1:T(1,128)S(1)} all-reduce(f32[32,1]{0,1:T(1,128)S(1)} %bitcast.54), channel_id=1, replica_groups=mesh['pipe'=16,'mp'=8] {'mp'}, use_global_device_ids=true, to_apply=%region_13.14 | all-reduce | flops 32 | bytes 256 | tf_op jit(solution)/shard_map/psum | solution.py:54
  422.5 0.7 fusion.11
  423.2 0.1 multiply_reduce_fusion
  423.3 12.5 %psum.47 = f32[32,1]{0,1:T(1,128)S(1)} all-reduce(f32[32,1]{0,1:T(1,128)S(1)} %bitcast.55), channel_id=1, replica_groups=mesh['pipe'=16,'mp'=8] {'mp'}, use_global_device_ids=true, to_apply=%region_15.16 | all-reduce | flops 32 | bytes 256 | tf_op jit(solution)/shard_map/psum | solution.py:57
  435.8 0.1 fusion.5
  435.9 13.6 %all-gather.1 = bf16[8,576,32]{1,2,0:T(8,128)(2,1)S(1)} all-gather(bf16[1,576,32]{1,2,0:T(8,128)(2,1)S(1)} %fusion.5), channel_id=1, replica_groups=mesh['pipe'=16,'mp'=8] {'mp'}, dimensions={0}, use_global_device_ids=true | all-gather | bytes 331776 | tf_op jit(solution)/shard_map/all_gather | solution.py:61
  449.4 0.1 copy.15
  449.5 0.2 reshape.21
  449.8 5.0 convolution_bitcast_fusion
  454.8 0.0 slice-start
  454.8 0.0 reduce-scatter.11.cloned.1.call-update
  454.9 0.6 subtract_reduce_fusion
  456.1 0.0 slice-start.1
  456.1 10.3 %convolution_convert_fusion = bf16[4608,1024]{1,0:T(8,128)(2,1)} fusion(bf16[512,4608]{1,0:T(8,128)(2,1)} %all-gather.7.cloned.1.call-done, f32[512,1024]{1,0:T(8,128)S(1)} %get-tuple-element.15, f32[512]{0:T(512)S(1)} %get-tuple-element.8, s32[1024]{0:T(1024)S(1)} %iota_add_fusion, s32[512]{0:T(512)S(1)} %copy-done.2), kind=kOutput, calls=%fused_computation | convolution fusion | flops 4841275392 | bytes 16261120 | tf_op jit(solution)/shard_map/dot_general | solution.py:43
  466.5 0.0 slice-done
  466.5 0.0 slice-done.1
  466.5 1.5 convolution_convert_fusion.1
  468.0 72.5 %reduce-scatter.11.cloned.1.call-done = f32[512,288]{0,1:T(8,128)} async-done(((f32[512,4608]{0,1:T(8,128)}), f32[512,288]{0,1:T(8,128)}) %reduce-scatter.11.cloned.1.call-update) | async-done | bytes 589840 | tf_op jit(solution)/shard_map/reduce_scatter | solution.py:67
  540.5 1.8 convert_element_type.33
  (6 shorter events, 0.0 us)
Async XLA Ops:
  7.2 60.1 %copy-start = (bf16[32,512]{1,0:T(8,128)(2,1)S(1)}, bf16[32,512]{1,0:T(8,128)(2,1)}, u32[]{:S(2)}) copy-start(bf16[32,512]{1,0:T(8,128)(2,1)} %param.7) | copy-start | bytes 98308
  7.2 60.1 %all-gather.5.cloned.1.call-start = ((), (), s32[]{:S(2)}) async-start(), calls=%async_computation.4 | async-start | bytes 5013504 | tf_op jit(solution)/shard_map/all_gather | solution.py:17
  7.9 95.6 %reduce-scatter.13.cloned.1.call-start = ((), (), s32[]{:S(2)}) async-start(), calls=%async_computation.8 | async-start | bytes 2654208
  72.4 47.9 %copy-start.1 = (bf16[32,576]{1,0:T(8,128)(2,1)S(1)}, bf16[32,576]{1,0:T(8,128)(2,1)}, u32[]{:S(2)}) copy-start(bf16[32,576]{1,0:T(8,128)(2,1)} %param.8) | copy-start | bytes 110596
  72.4 128.4 %copy-start.2 = (s32[512]{0:T(512)S(1)}, s32[512]{0:T(512)}, u32[]{:S(2)}) copy-start(s32[512]{0:T(512)} %param.13) | copy-start | bytes 6148
  72.4 128.4 %all-gather.7.cloned.1.call-start = ((), (), s32[]{:S(2)}) async-start(), calls=%async_computation.5 | async-start | bytes 5013504 | tf_op jit(solution)/shard_map/all_gather | solution.py:29
  147.7 223.1 %reduce-scatter.9.cloned.1.call-start = ((), (), s32[]{:S(2)}) async-start(), calls=%async_computation.6 | async-start | bytes 10027008 | tf_op jit(solution)/shard_map/reduce_scatter | solution.py:46
  287.1 118.4 %reduce-scatter.15.cloned.1.call-start = ((), (), s32[]{:S(2)}) async-start(), calls=%async_computation.9 | async-start | bytes 2654208
  373.9 166.6 %reduce-scatter.11.cloned.1.call-start = ((), (), s32[]{:S(2)}) async-start(), calls=%async_computation.7 | async-start | bytes 10027008 | tf_op jit(solution)/shard_map/reduce_scatter | solution.py:67
  454.8 11.6 %slice-start = ((s8[4718592]{0:T(1024)(128)(4,1)}), s8[524288]{0:T(1024)(128)(4,1)S(1)}, s32[]{:S(2)}) async-start(s8[4718592]{0:T(1024)(128)(4,1)} %bitcast.46), calls=%async_computation.10 | async-start | bytes 1048576
  456.1 10.3 %slice-start.1 = ((s8[4718592]{0:T(1024)(128)(4,1)}), s8[4194304]{0:T(1024)(128)(4,1)S(1)}, s32[]{:S(2)}) async-start(s8[4718592]{0:T(1024)(128)(4,1)} %bitcast.46), calls=%async_computation.11 | async-start | bytes 8388608
Sparse Core Ops, SparseCore 0:
  10.2 57.0 all-gather.4
  72.5 30.9 reduce-scatter.12
  147.8 53.0 all-gather.6
  287.3 83.4 reduce-scatter.8
  374.0 31.4 reduce-scatter.14
  455.0 85.4 reduce-scatter.10
where the time goes:
time: 551 us; the launch traced here: 550 us
  waiting for transfers between devices  330 us (60%)
  blocking collectives  148 us (27%)
  matrix products  43.5 us (8%)
  between operations  16 us (3%)
  local copies, waits for them, and re-layouts  8.31 us (2%)
    reduce_scatter x1, waiting for transfers between devices, on_device(): lax.psum_scatter(jnp.dot(logit_grad, head_weight.T, preferred_element_typ...  83.5 us
    reduce_scatter x1, waiting for transfers between devices, on_device(): lax.psum_scatter(o_term, 'pipe', scatter_dimension=1, tiled=True)  72.5 us
    psum x1, blocking collectives, on_device(): totals, target_logit = lax.psum((part_total, part_target), ('pipe', 'mp'))  64.8 us
    unnamed x8, waiting for transfers between devices  61.8 us
    all_gather x1, waiting for transfers between devices, on_device(): o_full = lax.all_gather(o_weight, 'pipe', axis=1, tiled=True)  59.3 us
    all_gather x1, waiting for transfers between devices, on_device(): all_rows = lax.all_gather(normed, 'pipe', axis=0, tiled=True)  53.1 us
    psum x1, blocking collectives, on_device(): lax.psum(jnp.sum(stream * upstream_grad, axis=-1, keepdims=True), 'mp')  15.7 us
    psum x1, blocking collectives, on_device(): lax.psum(jnp.sum(attn_share * attn_share, axis=-1, keepdims=True), 'mp')  15.6 us
  transfers between devices with their start and end apart: 6, of which 6 were waited for; matrix products, arithmetic and copies ran while one was open for 3% of the time, Pallas kernels for 0%

commit v1 on v0

v1 whole, which is shorter than its diff:
```python
import jax
import jax.numpy as jnp
from jax import lax
from jax.experimental import pallas as pl
from jax.experimental.pallas import tpu as pltpu
from jax.sharding import PartitionSpec as P

epsilon = 1e-06
softcap = 30.0
MESH = pl.DeviceIdType.MESH
F32, BF16 = jnp.float32, jnp.bfloat16

WIDTH = 4608
SHARE = 1152
PANELS = 9
COLS = 288
GATHER = (("z", "x", "y"), ("x", "y", "z"), ("y", "z", "x"))
NEAR = (1, 3, 2)


def remote(src, dst, send, recv, device):
    return pltpu.make_async_remote_copy(
        src_ref=src, dst_ref=dst, send_sem=send, recv_sem=recv, device_id=device, device_id_type=MESH
    )


def place(at):
    return (at["y"] * 4 + at["x"], at["z"] * 2 + at["c"])


def moved(at, dim, by):
    size = 2 if dim == "c" else 4
    return {**at, dim: lax.rem(at[dim] + by, size)}


def lanes(start, size):
    return pl.ds(pl.multiple_of(start, 128), size)


def rows_of(start, size):
    return pl.ds(pl.multiple_of(start, 16), size)


def section(
    ctx_ref, res_ref, ow_ref, pg_ref, fg_ref, w_hbm, tgt_ref,
    n_out, g_out, loss_out, og_out, dres_out, dctx_out,
    wv, ctx, ow, rres, aout, ain, attn_s, stream_s, nbuf, gath, cap, tgt, hot, part, psrc, pipe_in, mp_in, scale, grad,
    keep, sib_out, sib_in, first, r1a, r1b, r1c, s2, own2, r2a, r2b, r2c, s3, r3,
    gsum, cbuf, gout, gin, dcs, dcr, ogs, ogr, dsend, drecv,
    w_sem, ctx_ss, ctx_rs, sib_ss, sib_rs, at_ss, at_rs, z_ss, z_rs, ag_ss, ag_rs, agc_ss, agc_rs, tp_ss, tp_rs, tm_ss, tm_rs,
    rc_ss, rc_rs, rs_ss, rs_rs, ga_ss, ga_rs, dc_ss, dc_rs, out_sem,
):
    p, m = lax.axis_index("pipe"), lax.axis_index("mp")
    y, x, z, c = p // 4, p % 4, m // 2, m % 2
    at = {"y": y, "x": x, "z": z, "c": c}
    sib = (p, z * 2 + (1 - c))
    me = p * 2 + c
    peer32 = lambda j: lax.rem(me + j, 32)
    place32 = lambda i: (i // 2, z * 2 + i % 2)

    w_copies = [
        pltpu.make_async_copy(w_hbm.at[i], wv.at[:, pl.ds(i * 128, 128), :], w_sem.at[i]) for i in range(4)
    ]
    for copy in w_copies:
        copy.start()

    barrier = pltpu.get_barrier_semaphore()

    def greet(device):
        pl.semaphore_signal(barrier, inc=1, device_id=device, device_id_type=MESH)

    def greet32(j, _):
        greet(place32(peer32(j)))
        return 0

    lax.fori_loop(1, 32, greet32, 0)
    for by in (1, 2, 3):
        zz = lax.rem(z + by, 4)
        for cc in (0, 1):
            greet((p, zz * 2 + cc))
        for xx in range(4):
            greet((z * 4 + xx, zz * 2 + c))

    @pl.when(y != z)
    def _():
        def greet16(i, _):
            greet((i, y * 2 + c))
            return 0

        lax.fori_loop(0, 16, greet16, 0)

    pl.semaphore_wait(barrier, 49 + 16 * jnp.where(y != z, 1, 0))

    my_lanes = lanes(c * 512, 512)

    def ctx_send(j, _):
        i = peer32(j)
        remote(
            ctx_ref.at[rows_of((i % 2) * 16, 16)], ctx.at[p, :, my_lanes], ctx_ss.at[j], ctx_rs.at[j], place32(i)
        ).start()
        return 0

    lax.fori_loop(1, 32, ctx_send, 0)
    half = rows_of(c * 512, 512)
    ow_copy = remote(ow_ref, ow.at[half], sib_ss.at[0], sib_rs.at[0], sib)
    ow_copy.start()
    res_copy = remote(res_ref.at[rows_of((1 - c) * 16, 16)], rres, sib_ss.at[1], sib_rs.at[1], sib)
    res_copy.start()
    ctx[p, :, my_lanes] = ctx_ref[rows_of(c * 16, 16), :]
    ow[half, :] = ow_ref[...]
    for i in range(4):
        block = jnp.broadcast_to(tgt_ref[i : i + 1, :], (128, 128)).T
        for j in range(4):
            for cc in range(2):
                tgt[cc * 256 + (i * 4 + j) * 16 : cc * 256 + (i * 4 + j + 1) * 16, :] = block[
                    j * 32 + cc * 16 : j * 32 + (cc + 1) * 16, :
                ]

    def ctx_wait(j, _):
        i = lax.rem(me + 32 - j, 32)
        dst = ctx.at[i // 2, :, lanes((i % 2) * 512, 512)]
        remote(dst, dst, ctx_ss.at[j], ctx_rs.at[j], place32(i)).wait_recv()
        return 0

    lax.fori_loop(1, 32, ctx_wait, 0)
    remote(ow.at[rows_of((1 - c) * 512, 512)], ow.at[rows_of((1 - c) * 512, 512)], sib_ss.at[0], sib_rs.at[0], sib).wait_recv()

    aout[...] = jnp.dot(
        ctx[...].reshape(256, 1024), ow[...], preferred_element_type=F32
    ).reshape(16, 16, COLS)

    def attn_send(i, _):
        home = jnp.logical_and(i == p, y == z)

        @pl.when(jnp.logical_not(home))
        def _():
            remote(aout.at[i], ain.at[x, z], at_ss.at[i], at_rs.at[x, z], (i, y * 2 + c)).start()

        @pl.when(home)
        def _():
            ain[x, z] = aout[i]

        return 0

    lax.fori_loop(0, 16, attn_send, 0)
    res_copy.wait_recv()

    def attn_wait(i, _):
        xx, zz = i // 4, i % 4
        home = jnp.logical_and(jnp.logical_and(xx == x, zz == z), y == z)

        @pl.when(jnp.logical_not(home))
        def _():
            remote(ain.at[xx, zz], ain.at[xx, zz], at_ss.at[0], at_rs.at[xx, zz], (z * 4 + xx, zz * 2 + c)).wait_recv()

        return 0

    lax.fori_loop(0, 16, attn_wait, 0)
    attn = jnp.concatenate([ain[i, 0] + ain[i, 1] + ain[i, 2] + ain[i, 3] for i in range(4)], axis=1)
    mine, other = res_ref[rows_of(c * 16, 16), :].astype(F32), rres[...].astype(F32)
    residual = jnp.where(c == 0, jnp.concatenate([mine, other], axis=1), jnp.concatenate([other, mine], axis=1))
    share = lanes(z * SHARE, SHARE)
    post, final = pg_ref[:, share], fg_ref[:, share]

    def z_sum(which, value):
        nbuf[which, z] = value
        for by in NEAR:
            remote(
                nbuf.at[which, z], nbuf.at[which, z], z_ss.at[which, by - 1], z_rs.at[which, by - 1],
                place(moved(at, "z", by)),
            ).start()
        for by in NEAR:
            src = nbuf.at[which, lax.rem(z + 4 - by, 4)]
            remote(src, src, z_ss.at[which, by - 1], z_rs.at[which, by - 1], place(moved(at, "z", 4 - by))).wait_recv()
        return nbuf[which, 0] + nbuf[which, 1] + nbuf[which, 2] + nbuf[which, 3]

    def row_sum(value):
        return jnp.broadcast_to(jnp.sum(value, axis=1, keepdims=True), (16, 128))

    attn_sq = z_sum(0, row_sum(attn * attn))[:, :1]
    inv_attn = lax.rsqrt(attn_sq / WIDTH + epsilon)
    stream = residual + attn * inv_attn * post
    stream_sq = z_sum(1, row_sum(stream * stream))[:, :1]
    inv_stream = lax.rsqrt(stream_sq / WIDTH + epsilon)
    normed = (stream * inv_stream * final).astype(BF16)
    attn_s[...] = attn
    stream_s[...] = stream
    nbuf[4, 0] = jnp.broadcast_to(inv_attn, (16, 128))
    nbuf[4, 1] = jnp.broadcast_to(inv_stream, (16, 128))

    my_z = lanes(z * 128, 128)
    for q in range(PANELS):
        gath[q, c, y, x, :, my_z] = normed[:, q * 128 : (q + 1) * 128]

    def region(q, here, done):
        return gath.at[
            q,
            here["c"],
            pl.ds(0, 4) if "y" in done else here["y"],
            pl.ds(0, 4) if "x" in done else here["x"],
            :,
            pl.ds(0, 512) if "z" in done else lanes(here["z"] * 128, 128),
        ]

    def ag_start(q, stage):
        dims = GATHER[q % 3]
        src = region(q, at, dims[:stage])
        for by in NEAR:
            remote(
                src, src, ag_ss.at[q, stage, by - 1], ag_rs.at[q, stage, by - 1], place(moved(at, dims[stage], by))
            ).start()

    def ag_wait(q, stage):
        dims = GATHER[q % 3]
        for by in NEAR:
            source = moved(at, dims[stage], 4 - by)
            src = region(q, source, dims[:stage])
            remote(src, src, ag_ss.at[q, stage, by - 1], ag_rs.at[q, stage, by - 1], place(source)).wait_recv()

    for q in range(PANELS):
        ag_start(q, 0)
    for stage in (1, 2):
        for q in range(PANELS):
            ag_wait(q, stage - 1)
            ag_start(q, stage)
    for copy in w_copies:
        copy.wait()

    def logits(third, which):
        rows = lambda: rows_of(which * 256, 256)

        @pl.loop(0, 4)
        def _(block):
            cols = lanes(block * 256, 256)
            total = None
            for q in range(third * 3, third * 3 + 3):
                term = jnp.dot(gath[q, which].reshape(256, 512), wv[q, :, cols], preferred_element_type=F32)
                total = term if total is None else total + term
            if third > 0:
                total = total + cap[rows(), cols]
            if third < 2:
                cap[rows(), cols] = total
            else:
                capped = softcap * jnp.tanh(total * (1.0 / softcap))
                cap[rows(), cols] = capped
                expd = jnp.exp(capped)
                first_col = m * 1024 + p * 8192 + block * 256
                ids = lax.broadcasted_iota(jnp.int32, (256, 128), 1) + first_col
                wanted = tgt[rows(), :]
                sums = expd[:, :128] + expd[:, 128:]
                hits = jnp.where(ids == wanted, capped[:, :128], 0.0) + jnp.where(
                    ids + 128 == wanted, capped[:, 128:], 0.0
                )

                @pl.when(block == 0)
                def _():
                    part[rows(), :] = sums
                    hot[rows(), :] = hits

                @pl.when(block > 0)
                def _():
                    part[rows(), :] += sums
                    hot[rows(), :] += hits

    for third in range(3):
        for q in range(third * 3, third * 3 + 3):
            ag_wait(q, 2)
            remote(gath.at[q, c], gath.at[q, c], agc_ss.at[q], agc_rs.at[q], sib).start()
        logits(third, c)
        for q in range(third * 3, third * 3 + 3):
            remote(gath.at[q, 1 - c], gath.at[q, 1 - c], agc_ss.at[q], agc_rs.at[q], sib).wait_recv()
        logits(third, 1 - c)
    n_copy = pltpu.make_async_copy(gath, n_out, out_sem.at[0])
    n_copy.start()

    for i in range(4):
        psrc[i : i + 1, :] = jnp.sum(part[i * 128 : (i + 1) * 128, :].T, axis=0, keepdims=True)
        psrc[i + 4 : i + 5, :] = jnp.sum(hot[i * 128 : (i + 1) * 128, :].T, axis=0, keepdims=True)
    pipe_in[p] = psrc[...]

    def pipe_send(j, _):
        remote(psrc, pipe_in.at[p], tp_ss.at[j], tp_rs.at[j], (lax.rem(p + j, 16), m)).start()
        return 0

    def pipe_wait(j, _):
        i = lax.rem(p + 16 - j, 16)
        remote(psrc, pipe_in.at[i], tp_ss.at[j], tp_rs.at[j], (i, m)).wait_recv()
        return 0

    lax.fori_loop(1, 16, pipe_send, 0)
    lax.fori_loop(1, 16, pipe_wait, 0)
    mp_in[m] = jnp.sum(pipe_in[...], axis=0)

    def mp_send(j, _):
        remote(mp_in.at[m], mp_in.at[m], tm_ss.at[j], tm_rs.at[j], (p, lax.rem(m + j, 8))).start()
        return 0

    def mp_wait(j, _):
        i = lax.rem(m + 8 - j, 8)
        remote(mp_in.at[i], mp_in.at[i], tm_ss.at[j], tm_rs.at[j], (p, i)).wait_recv()
        return 0

    lax.fori_loop(1, 8, mp_send, 0)
    lax.fori_loop(1, 8, mp_wait, 0)
    sums = jnp.sum(mp_in[...], axis=0)
    totals, target_logit = sums[:4], sums[4:]
    loss_out[...] = jnp.sum(
        jnp.sum(jnp.log(totals) - target_logit, axis=0, keepdims=True), axis=1, keepdims=True
    ) * (1.0 / 512)
    inverse = 1.0 / totals
    for i in range(4):
        scale[i * 128 : (i + 1) * 128, :] = jnp.broadcast_to(inverse[i : i + 1, :], (128, 128)).T

    @pl.loop(0, 16)
    def _(block):
        rows = rows_of(block * 32, 32)
        wanted, inv = tgt[rows, :], scale[rows, :]
        ids = lax.broadcasted_iota(jnp.int32, (32, 128), 1) + (m * 1024 + p * 8192)
        for j in range(8):
            cols = slice(j * 128, (j + 1) * 128)
            capped = cap[rows, cols]
            ratio = capped * (1.0 / softcap)
            hit = jnp.where(ids + j * 128 == wanted, 1.0, 0.0)
            grad[rows, cols] = ((jnp.exp(capped) * inv - hit) * (1.0 - ratio * ratio)).astype(BF16)

    g_copy = pltpu.make_async_copy(grad, g_out, out_sem.at[1])
    g_copy.start()

    def grad_dot(q, which):
        rows = rows_of(which * 256, 256)
        return lax.dot_general(grad[rows, :], wv[q], (((1,), (1,)), ((), ())), preferred_element_type=F32).reshape(
            4, 4, 16, 512
        )

    def rs_sib(q):
        sib_out[q] = grad_dot(q, 1 - c).astype(BF16)
        remote(sib_out.at[q], sib_in.at[q], rc_ss.at[q], rc_rs.at[q], sib).start()

    def piece(ref, dim, index, left, lead):
        where = list(lead)
        for d in ("y", "x"):
            if d in left:
                where.append(index if d == dim else pl.ds(0, 4))
        where.append(pl.ds(0, 16))
        if "z" in left:
            where.append(lanes(index * 128, 128) if dim == "z" else pl.ds(0, 512))
        else:
            where.append(pl.ds(0, 128))
        return tuple(where)

    r1 = (r1a, r1b, r1c)
    r2 = (r2a, r2b, r2c)
    dims_of = lambda q: GATHER[q % 3][::-1]

    def rs_first(q):
        remote(sib_out.at[q], sib_in.at[q], rc_ss.at[q], rc_rs.at[q], sib).wait_recv()
        total = keep[q] + sib_in[q].astype(F32)
        keep[q] = total
        first[q] = total.astype(BF16)
        dim = dims_of(q)[0]
        for by in NEAR:
            there = moved(at, dim, by)
            src = first.at[piece(first, dim, there[dim], ("y", "x", "z"), (q,))]
            remote(src, r1[q % 3].at[q // 3, by - 1], rs_ss.at[q, 0, by - 1], rs_rs.at[q, 0, by - 1], place(there)).start()

    def rs_recv(q, stage, ref):
        dim = dims_of(q)[stage]
        for by in NEAR:
            dst = ref.at[by - 1]
            remote(
                dst, dst, rs_ss.at[q, stage, by - 1], rs_rs.at[q, stage, by - 1], place(moved(at, dim, 4 - by))
            ).wait_recv()

    def rs_second(q):
        k, r = q % 3, q // 3
        got = r1[k].at[r]
        rs_recv(q, 0, got)
        dims = dims_of(q)
        left = [d for d in ("y", "x", "z") if d != dims[0]]
        total = keep[piece(keep, dims[0], at[dims[0]], ("y", "x", "z"), (q,))]
        total = total + got[0].astype(F32) + got[1].astype(F32) + got[2].astype(F32)
        own2[k][r] = total
        s2[k][r] = total.astype(BF16)
        for by in NEAR:
            there = moved(at, dims[1], by)
            src = s2[k].at[piece(s2[k], dims[1], there[dims[1]], left, (r,))]
            remote(src, r2[k].at[r, by - 1], rs_ss.at[q, 1, by - 1], rs_rs.at[q, 1, by - 1], place(there)).start()

    def rs_third(q):
        k, r = q % 3, q // 3
        got = r2[k].at[r]
        rs_recv(q, 1, got)
        dims = dims_of(q)
        left = [d for d in ("y", "x", "z") if d != dims[0]]
        total = own2[k][piece(own2[k], dims[1], at[dims[1]], left, (r,))]
        total = total + got[0].astype(F32) + got[1].astype(F32) + got[2].astype(F32)
        s3[k][r] = total
        for by in NEAR:
            there = moved(at, dims[2], by)
            src = s3[k].at[piece(s3[k], dims[2], there[dims[2]], [dims[2]], (r,))]
            remote(src, r3.at[q, by - 1], rs_ss.at[q, 2, by - 1], rs_rs.at[q, 2, by - 1], place(there)).start()

    def rs_last(q):
        k, r = q % 3, q // 3
        rs_recv(q, 2, r3.at[q])
        dims = dims_of(q)
        own = s3[k][piece(s3[k], dims[2], at[dims[2]], [dims[2]], (r,))]
        gsum[:, q * 128 : (q + 1) * 128] = own + r3[q, 0] + r3[q, 1] + r3[q, 2]

    rs_sib(0)
    for q in range(PANELS):
        keep[q] = grad_dot(q, c)
        if q + 1 < PANELS:
            rs_sib(q + 1)
        rs_first(q)
    for q in range(PANELS):
        rs_second(q)
    for q in range(PANELS):
        rs_third(q)
    for q in range(PANELS):
        rs_last(q)

    stream, attn = stream_s[...], attn_s[...]
    inv_attn, inv_stream = nbuf[4, 0][:, :1], nbuf[4, 1][:, :1]
    post, final = pg_ref[:, share], fg_ref[:, share]
    upstream = gsum[...] * final
    cross = z_sum(2, row_sum(stream * upstream))[:, :1]
    grad_stream = inv_stream * (upstream - stream * (inv_stream * inv_stream) * (cross / WIDTH))
    scaled = grad_stream * post
    cross_attn = z_sum(3, row_sum(attn * scaled))[:, :1]
    grad_attn = (inv_attn * (scaled - attn * (inv_attn * inv_attn) * (cross_attn / WIDTH))).astype(BF16)
    for i in range(4):
        gout[i] = grad_attn[:, i * COLS : (i + 1) * COLS]

    def ga_send(i, _):
        xx, zz = i // 4, i % 4
        home = jnp.logical_and(jnp.logical_and(xx == x, zz == z), y == z)

        @pl.when(jnp.logical_not(home))
        def _():
            remote(gout.at[xx], gin.at[p], ga_ss.at[i], ga_rs.at[p], (z * 4 + xx, zz * 2 + c)).start()

        @pl.when(home)
        def _():
            gin[p] = gout[xx]

        return 0

    lax.fori_loop(0, 16, ga_send, 0)
    d_res = grad_stream.astype(BF16)
    left_half, right_half = d_res[:, :576], d_res[:, 576:]
    dsend[...] = jnp.where(c == 0, right_half, left_half)
    dres_copy = remote(dsend, drecv, sib_ss.at[2], sib_rs.at[2], sib)
    dres_copy.start()
    dres_out[rows_of(c * 16, 16), :] = jnp.where(c == 0, left_half, right_half)

    def ga_wait(i, _):
        home = jnp.logical_and(i == p, y == z)

        @pl.when(jnp.logical_not(home))
        def _():
            remote(gin.at[i], gin.at[i], ga_ss.at[0], ga_rs.at[i], (i, y * 2 + c)).wait_recv()

        return 0

    lax.fori_loop(0, 16, ga_wait, 0)
    ga = gin[...].reshape(256, COLS)
    dcs[...] = (
        lax.dot_general(ga, ow[...], (((1,), (1,)), ((), ())), preferred_element_type=F32)
        .astype(BF16)
        .reshape(16, 16, 1024)
    )

    def dc_send(j, _):
        i = peer32(j)
        remote(
            dcs.at[i // 2, :, lanes((i % 2) * 512, 512)], dcr.at[me], dc_ss.at[j], dc_rs.at[j], place32(i)
        ).start()
        return 0

    lax.fori_loop(1, 32, dc_send, 0)
    dcr[me] = dcs[p, :, my_lanes]

    def og_dot(which):
        heads = ctx[:, :, lanes(which * 512, 512)].reshape(256, 512)
        return lax.dot_general(heads, ga, (((0,), (0,)), ((), ())), preferred_element_type=F32)

    ogs[...] = og_dot(1 - c)
    og_copy = remote(ogs, ogr, sib_ss.at[3], sib_rs.at[3], sib)
    og_copy.start()
    og_own = og_dot(c)
    og_copy.wait_recv()
    og_out[...] = (og_own + ogr[...]).astype(BF16)
    dres_copy.wait_recv()
    dres_out[rows_of((1 - c) * 16, 16), :] = drecv[...]

    def dc_wait(j, _):
        i = lax.rem(me + 32 - j, 32)
        remote(dcr.at[i], dcr.at[i], dc_ss.at[j], dc_rs.at[j], place32(i)).wait_recv()
        return 0

    lax.fori_loop(1, 32, dc_wait, 0)
    for cc in range(2):
        total = dcr[cc].astype(F32)
        for i in range(1, 16):
            total = total + dcr[2 * i + cc].astype(F32)
        dctx_out[cc * 16 : (cc + 1) * 16, :] = total.astype(BF16)

    def ctx_sent(j, _):
        src = ctx_ref.at[pl.ds(0, 16)]
        remote(src, src, ctx_ss.at[j], ctx_rs.at[j], sib).wait_send()
        src = dcr.at[0]
        remote(src, src, dc_ss.at[j], dc_rs.at[j], sib).wait_send()
        return 0

    lax.fori_loop(1, 32, ctx_sent, 0)

    def at_sent(i, _):
        @pl.when(jnp.logical_not(jnp.logical_and(i == p, y == z)))
        def _():
            remote(aout.at[i], aout.at[i], at_ss.at[i], at_rs.at[0, 0], sib).wait_send()

        @pl.when(jnp.logical_not(jnp.logical_and(jnp.logical_and(i // 4 == x, i % 4 == z), y == z)))
        def _():
            remote(gout.at[0], gout.at[0], ga_ss.at[i], ga_rs.at[0], sib).wait_send()

        return 0

    lax.fori_loop(0, 16, at_sent, 0)

    def tp_sent(j, _):
        remote(psrc, psrc, tp_ss.at[j], tp_rs.at[j], sib).wait_send()
        return 0

    lax.fori_loop(1, 16, tp_sent, 0)

    def tm_sent(j, _):
        remote(psrc, psrc, tm_ss.at[j], tm_rs.at[j], sib).wait_send()
        return 0

    lax.fori_loop(1, 8, tm_sent, 0)
    ow_copy.wait_send()
    res_copy.wait_send()
    dres_copy.wait_send()
    og_copy.wait_send()
    for which in range(4):
        for by in NEAR:
            remote(nbuf.at[0, 0], nbuf.at[0, 0], z_ss.at[which, by - 1], z_rs.at[which, by - 1], sib).wait_send()
    for q in range(PANELS):
        k, r = q % 3, q // 3
        remote(gath.at[q, c], gath.at[q, c], agc_ss.at[q], agc_rs.at[q], sib).wait_send()
        remote(sib_out.at[q], sib_in.at[q], rc_ss.at[q], rc_rs.at[q], sib).wait_send()
        for by in NEAR:
            for stage in range(3):
                src = region(q, at, GATHER[k][:stage])
                remote(src, src, ag_ss.at[q, stage, by - 1], ag_rs.at[q, stage, by - 1], sib).wait_send()
                src = (r1[k].at[r, 0], r2[k].at[r, 0], r3.at[q, 0])[stage]
                remote(src, src, rs_ss.at[q, stage, by - 1], rs_rs.at[q, stage, by - 1], sib).wait_send()
    n_copy.wait()
    g_copy.wait()


def section_listed(*refs):
    ins, outs, rest = refs[:7], refs[7:13], refs[13:]
    names, n = [], 0
    for count in LAYOUT:
        names.append(rest[n] if count == 1 else tuple(rest[n : n + count]))
        n += count
    section(*ins, *outs, *names)


VM = pltpu.VMEM
DMA = pltpu.SemaphoreType.DMA
SCRATCH = [
    VM((9, 512, 1024), BF16),
    VM((16, 16, 1024), BF16),
    VM((1024, COLS), BF16),
    VM((16, 576), BF16),
    VM((16, 16, COLS), F32),
    VM((4, 4, 16, COLS), F32),
    VM((16, SHARE), F32),
    VM((16, SHARE), F32),
    VM((5, 4, 16, 128), F32),
    VM((9, 2, 4, 4, 16, 512), BF16),
    VM((512, 1024), F32),
    VM((512, 128), jnp.int32),
    VM((512, 128), F32),
    VM((512, 128), F32),
    VM((8, 128), F32),
    VM((16, 8, 128), F32),
    VM((8, 8, 128), F32),
    VM((512, 128), F32),
    VM((512, 1024), BF16),
    VM((9, 4, 4, 16, 512), F32),
    VM((9, 4, 4, 16, 512), BF16),
    VM((9, 4, 4, 16, 512), BF16),
    VM((9, 4, 4, 16, 512), BF16),
    VM((3, 3, 4, 16, 512), BF16),
    VM((3, 3, 4, 4, 16, 128), BF16),
    VM((3, 3, 4, 16, 512), BF16),
    (VM((3, 4, 16, 512), BF16), VM((3, 4, 4, 16, 128), BF16), VM((3, 4, 16, 512), BF16)),
    (VM((3, 4, 16, 512), F32), VM((3, 4, 4, 16, 128), F32), VM((3, 4, 16, 512), F32)),
    VM((3, 3, 16, 512), BF16),
    VM((3, 3, 4, 16, 128), BF16),
    VM((3, 3, 4, 16, 128), BF16),
    (VM((3, 16, 512), F32), VM((3, 4, 16, 128), F32), VM((3, 4, 16, 128), F32)),
    VM((9, 3, 16, 128), F32),
    VM((16, SHARE), F32),
    VM((8, 128), F32),
    VM((4, 16, COLS), BF16),
    VM((16, 16, COLS), BF16),
    VM((16, 16, 1024), BF16),
    VM((32, 16, 512), BF16),
    VM((512, COLS), F32),
    VM((512, COLS), F32),
    VM((16, 576), BF16),
    VM((16, 576), BF16),
    DMA((4,)),
    DMA((32,)), DMA((32,)),
    DMA((4,)), DMA((4,)),
    DMA((16,)), DMA((4, 4)),
    DMA((4, 3)), DMA((4, 3)),
    DMA((9, 3, 3)), DMA((9, 3, 3)),
    DMA((9,)), DMA((9,)),
    DMA((16,)), DMA((16,)),
    DMA((8,)), DMA((8,)),
    DMA((9,)), DMA((9,)),
    DMA((9, 3, 3)), DMA((9, 3, 3)),
    DMA((16,)), DMA((16,)),
    DMA((32,)), DMA((32,)),
    DMA((2,)),
]
LAYOUT = [len(s) if type(s) is tuple else 1 for s in SCRATCH]
FLAT = [t for s in SCRATCH for t in (s if type(s) is tuple else (s,))]


def head_grad_kernel(n_ref, g_ref, loss_in, og_in, dres_in, dctx_in, hg_ref, loss_ref, og_ref, dres_ref, dctx_ref):
    product = lax.dot_general(n_ref[0], g_ref[...], (((0,), (0,)), ((), ())), preferred_element_type=F32)
    hg_ref[...] = product.astype(BF16).reshape(4, 1, 128, 1024)

    @pl.when(pl.program_id(0) == 0)
    def _():
        loss_ref[...] = loss_in[...]
        og_ref[...] = og_in[...]
        dres_ref[...] = dres_in[...]
        dctx_ref[...] = dctx_in[...]


def on_device(context, residual_in, o_weight, post_gain, final_gain, head_weight, targets):
    vmem, hbm = pl.BlockSpec(memory_space=pltpu.VMEM), pl.BlockSpec(memory_space=pl.ANY)
    shape = jax.ShapeDtypeStruct
    small = [shape((1, 1), F32), shape((512, COLS), BF16), shape((32, 576), BF16), shape((32, 512), BF16)]
    normed, grad, loss, og, dres, dctx = pl.pallas_call(
        section_listed,
        out_shape=[shape((9, 2, 4, 4, 16, 512), BF16), shape((512, 1024), BF16), *small],
        in_specs=[vmem, vmem, vmem, vmem, vmem, hbm, vmem],
        out_specs=[hbm, hbm, vmem, vmem, vmem, vmem],
        scratch_shapes=FLAT,
        compiler_params=pltpu.CompilerParams(
            collective_id=0, has_side_effects=True, vmem_limit_bytes=60 * 2**20
        ),
        cost_estimate=pl.CostEstimate(flops=10**10, bytes_accessed=20 * 10**6, transcendentals=10**6),
        name="section",
    )(
        context,
        residual_in,
        o_weight,
        post_gain.reshape(1, WIDTH),
        final_gain.reshape(1, WIDTH),
        head_weight.reshape(4, 9, 128, 1024),
        targets.reshape(4, 128),
    )
    whole = lambda *dims: pl.BlockSpec(dims, lambda q: (0,) * len(dims))
    head_grad, loss, og, dres, dctx = pl.pallas_call(
        head_grad_kernel,
        grid=(9,),
        out_shape=[shape((4, 9, 128, 1024), BF16), *small],
        in_specs=[
            pl.BlockSpec((1, 512, 512), lambda q: (q, 0, 0)),
            whole(512, 1024), whole(1, 1), whole(512, COLS), whole(32, 576), whole(32, 512),
        ],
        out_specs=[
            pl.BlockSpec((4, 1, 128, 1024), lambda q: (0, q, 0, 0)),
            whole(1, 1), whole(512, COLS), whole(32, 576), whole(32, 512),
        ],
        compiler_params=pltpu.CompilerParams(vmem_limit_bytes=48 * 2**20),
        cost_estimate=pl.CostEstimate(flops=5 * 10**9, bytes_accessed=16 * 10**6, transcendentals=0),
        name="head_grad",
    )(normed.reshape(9, 512, 512), grad, loss, og, dres, dctx)
    return (loss.reshape(()), head_grad.reshape(WIDTH, 1024), og, dres, dctx)


def solution(mesh):
    placed = (
        P("pipe", "mp"),
        P("pipe", "mp"),
        P("mp", "pipe"),
        P(),
        P(),
        P(None, ("pipe", "mp")),
        P(),
    )
    return jax.shard_map(
        on_device,
        mesh=mesh,
        in_specs=placed,
        out_specs=(P(), P(None, ("pipe", "mp")), P("mp", "pipe"), P("pipe", "mp"), P("pipe", "mp")),
        check_vma=False,
    )
```

time: 551 us -> 148 us (0.27)
  waiting for transfers between devices: 330 us -> 0 us
  blocking collectives: 148 us -> 0 us
  Pallas kernels: 0 us -> 137 us
  matrix products: 43.5 us -> 0 us
  between operations: 16 us -> 0.65 us
    reduce_scatter x2 -> x0, waiting for transfers between devices: 156 us -> none  [the longest x1 83.5 us: on_device(): lax.psum_scatter(jnp.dot(logit_grad, head_weight.T, preferred_element_typ...]
    pallas_call x0 -> x2, Pallas kernels: none -> 137 us  [the longest x1 125 us: on_device(): pl.pallas_call(section_listed, out_shape=[shape((9, 2, 4, 4, 16, 512), BF...]
    psum x5 -> x0, blocking collectives: 121 us -> none  [the longest x1 64.8 us: on_device(): totals, target_logit = lax.psum((part_total, part_target), ('pipe', 'mp'))]
    all_gather x2 -> x0, waiting for transfers between devices: 112 us -> none  [the longest x1 59.3 us: on_device(): o_full = lax.all_gather(o_weight, 'pipe', axis=1, tiled=True)]
    unnamed x8 -> x0, waiting for transfers between devices: 61.8 us -> none
    dot_general x5 -> x0, matrix products: 38.4 us -> none  [the longest x1 11.9 us: on_device(): jnp.dot(logit_grad, head_weight.T, preferred_element_type=jnp.float32)]
    all_gather x2 -> x0, blocking collectives: 27 us -> none  [the longest x1 13.6 us: on_device(): lax.all_gather(attn_grad_share.astype(jnp.bfloat16), 'mp', axis=1, tiled=...]
  transfers between devices with their start and end apart: 6 -> 0, of which waited for: 6 -> 0; matrix products, arithmetic and copies ran while one was open for 3% -> 0% of each run, Pallas kernels for 0% -> 0%
where the time goes in v1:
time: 148 us; the launch traced here: 147 us
  Pallas kernels  137 us (93%)
  local copies, waits for them, and re-layouts  9.2 us (6%)
    pallas_call x1, Pallas kernels, on_device(): pl.pallas_call(section_listed, out_shape=[shape((9, 2, 4, 4, 16, 512), BF...  125 us
    pallas_call x1, Pallas kernels, on_device(): pl.pallas_call(head_grad_kernel, grid=(9,), out_shape=[shape((4, 9, 128,...  12.2 us
    unnamed x10, local copies, waits for them, and re-layouts  6.51 us

profile of v1, /device:TPU:1, one launch (start us, length us, event | category | flops | bytes accessed | tf_op | source)
XLA Modules:
  0.0 147.0 jit_solution(1485420179041278449)
XLA Ops:
  0.6 1.3 reshape.31.refs_3_
  2.0 1.3 reshape.32.refs_4_
  3.3 1.9 %copy.12.refs_2_ = bf16[512,288]{1,0:T(8,128)(2,1)} copy(bf16[512,288]{0,1:T(8,128)(2,1)} %param.9) | data formatting | bytes 589824 | tf_op args[2]
  5.2 125.0 %section.1 = (bf16[9,2,4,4,16,512]{5,4,3,2,1,0:T(8,128)(2,1)}, bf16[512,1024]{1,0:T(8,128)(2,1)}, f32[1,1]{1,0:T(1,128)}, bf16[512,288]{1,0:T(8,128)(2,1)}, bf16...) custom-call(bf16[32,512]{1,0:T(8,128)(2,1)} %refs_0_.1, bf16[32,576]{1,0:T(8,128)(2,1)} %refs_1_.1, ...), custom_call_target="tpu_custom_call" | custom-call | flops 10000000000 | bytes 20000000 | tf_op jit(solution)/shard_map/section/pallas_call | solution.py:653
  130.2 0.0 copy-start
  130.2 1.2 copy-done
  131.4 0.0 copy-start.1
  131.4 1.0 copy-done.1
  132.4 0.0 copy-start.2
  132.4 0.8 copy-done.2
  133.2 0.0 copy-start.3
  133.2 0.8 copy-done.3
  133.9 12.2 %head_grad.1 = (bf16[4,9,128,1024]{3,2,1,0:T(8,128)(2,1)}, f32[1,1]{1,0:T(1,128)}, bf16[512,288]{1,0:T(8,128)(2,1)S(1)}, bf16[32,576]{1,0:T(8,128)(2,1)}, bf16[32,512]{1,0:T(8,128)(2,1)}) custom-call(bf16[9,512,512]{2,1,0:T(8,128)(2,1)} %bitcast.8, bf16[512,1024]{1,0:T(8,128)(2,1)S(1)} %copy-done, f32[1,1]{1,0:T(1,128)} %get-tuple-element.18.loss_in, ...), custom_call_target="tpu_custom_call" | custom-call | flops 5000000000 | bytes 16000000 | tf_op jit(solution)/shard_map/head_grad/pallas_call | solution.py:674
  146.1 0.9 copy.13
Async XLA Ops:
  130.2 1.2 copy-start
  131.4 1.0 copy-start.1
  132.4 0.8 copy-start.2
  133.2 0.8 copy-start.3

commit v2 on v1

v2 whole, which is shorter than its diff:
```python
import jax
import jax.numpy as jnp
from jax import lax
from jax.experimental import pallas as pl
from jax.experimental.pallas import tpu as pltpu
from jax.sharding import PartitionSpec as P

epsilon = 1e-06
softcap = 30.0
MESH = pl.DeviceIdType.MESH
F32, BF16 = jnp.float32, jnp.bfloat16

WIDTH = 4608
SHARE = 1152
PANELS = 9
CHUNK = 8
EARLY = 4
COLS = 288
GATHER = (("y", "x", "z"), ("x", "z", "y"), ("z", "y", "x"))
NEAR = (1, 3, 2)


def remote(src, dst, send, recv, device):
    return pltpu.make_async_remote_copy(
        src_ref=src, dst_ref=dst, send_sem=send, recv_sem=recv, device_id=device, device_id_type=MESH
    )


def place(at):
    return (at["y"] * 4 + at["x"], at["z"] * 2 + at["c"])


def moved(at, dim, by):
    size = 2 if dim == "c" else 4
    return {**at, dim: lax.rem(at[dim] + by, size)}


def lanes(start, size):
    return pl.ds(pl.multiple_of(start, 128), size)


def rows_of(start, size):
    return pl.ds(pl.multiple_of(start, 16), size)


def section(
    ctx_ref, res_ref, ow_ref, pg_ref, fg_ref, w_hbm, tgt_ref,
    n_out, g_out, x_out, loss_out, og_out, dres_out, dctx_out,
    wv, ctx, ow, pg, fg, rres, aout, ain, attn_s, stream_s, nbuf, gath, turned_q, cap, tgt, hot, part,
    psrc, pipe_in, mp_in, scale, grad, early,
    keep, sib_out, sib_in, first, r1a, r1b, r1c, s2, own2, r2a, r2b, r2c, s3, r3,
    gsum, gout, gin, dcs, dcr, ogs, ogr, dsend, drecv,
    w_sem, ctx_ss, ctx_rs, sib_ss, sib_rs, tn_ss, tn_rs, at_ss, at_rs, y_ss, y_rs, ag_ss, ag_rs, agc_ss, agc_rs, tp_ss, tp_rs, tm_ss, tm_rs,
    rc_ss, rc_rs, rs_ss, rs_rs, ga_ss, ga_rs, dc_ss, dc_rs, out_sem, early_sem,
):
    p, m = lax.axis_index("pipe"), lax.axis_index("mp")
    y, x, z, c = p // 4, p % 4, m // 2, m % 2
    at = {"y": y, "x": x, "z": z, "c": c}
    sib = (p, z * 2 + (1 - c))
    me = p * 2 + c
    peer32 = lambda j: lax.rem(me + j, 32)
    place32 = lambda i: (i // 2, z * 2 + i % 2)

    w_copies = [
        pltpu.make_async_copy(w_hbm.at[i], wv.at[:, pl.ds(i * 128, 128), :], w_sem) for i in range(4)
    ]
    for copy in w_copies:
        copy.start()

    pending = []

    def finish():
        for wait in pending:
            wait()

    def landed(like, sem):
        remote(like, like, sem, sem, sib).wait_recv()

    def gone(like, sem):
        pending.append(remote(like, like, sem, sem, sib).wait_send)

    barrier = pltpu.get_barrier_semaphore()

    def greet(device):
        pl.semaphore_signal(barrier, inc=1, device_id=device, device_id_type=MESH)

    def greet32(j, _):
        greet(place32(peer32(j)))
        return 0

    lax.fori_loop(1, 32, greet32, 0)
    for by in (1, 2, 3):
        zz = lax.rem(z + by, 4)
        greet((p, zz * 2 + (1 - c)))
        for xx in range(4):
            greet((y * 4 + xx, zz * 2 + c))
    turned = (z * 4 + x, y * 2)

    @pl.when(y != z)
    def _():
        for cc in range(2):
            greet((turned[0], turned[1] + cc))

    pl.semaphore_wait(barrier, 46 + 2 * jnp.where(y != z, 1, 0))

    my_lanes = lanes(c * 512, 512)

    def ctx_copy(by, h):
        there = lax.rem(p + by, 16)
        src = ctx_ref.at[rows_of(h * 16, 16)]
        return remote(src, ctx.at[p, :, my_lanes], ctx_ss.at[0], ctx_rs.at[by // CHUNK], (there, z * 2 + h))

    def ctx_send(by, _):
        for h in range(2):
            ctx_copy(by, h).start()
        return 0

    ctx_home = remote(
        ctx_ref.at[rows_of((1 - c) * 16, 16)], ctx.at[p, :, my_lanes], sib_ss.at[2], sib_rs.at[2], sib
    )
    ctx_home.start()
    pending.append(ctx_home.wait_send)
    ow_copy = remote(ow_ref, ow.at[:, my_lanes], sib_ss.at[0], sib_rs.at[0], sib)
    ow_copy.start()
    pending.append(ow_copy.wait_send)
    lax.fori_loop(1, 16, ctx_send, 0)
    gone(ctx.at[pl.ds(0, 15)], ctx_ss.at[0])

    def turn(sources, landing, base):
        def at_home(cc):
            return jnp.logical_and(y == z, c == cc)

        for cc in range(2):
            copy = remote(
                sources[cc], landing.at[c], tn_ss.at[base, cc], tn_rs.at[base, c], (turned[0], turned[1] + cc)
            )
            pl.when(jnp.logical_not(at_home(cc)))(copy.start)

            @pl.when(at_home(cc))
            def _(cc=cc):
                landing[cc] = sources[cc][...]

            pending.append(lambda cc=cc, copy=copy: pl.when(jnp.logical_not(at_home(cc)))(copy.wait_send))

        def receive():
            for cc in range(2):
                copy = remote(
                    landing.at[cc], landing.at[cc], tn_ss.at[base, cc], tn_rs.at[base, cc], (turned[0], turned[1] + cc)
                )
                pl.when(jnp.logical_not(at_home(cc)))(copy.wait_recv)

        return receive

    res_receive = turn([res_ref.at[pl.ds(cc * 16, 16)] for cc in range(2)], rres, 0)
    ctx[p, :, my_lanes] = ctx_ref[rows_of(c * 16, 16), :]
    ow[:, my_lanes] = ow_ref[...]
    pg[...] = pg_ref[...].reshape(1, WIDTH)
    fg[...] = fg_ref[...].reshape(1, WIDTH)
    for i in range(4):
        block = jnp.broadcast_to(tgt_ref[i : i + 1, :], (128, 128)).T
        for j in range(4):
            for cc in range(2):
                tgt[cc * 256 + (i * 4 + j) * 16 : cc * 256 + (i * 4 + j + 1) * 16, :] = block[
                    j * 32 + cc * 16 : j * 32 + (cc + 1) * 16, :
                ]

    ctx_there = ctx.at[p, :, lanes((1 - c) * 512, 512)]
    landed(ctx_there, sib_rs.at[2])
    ow_there = ow.at[:, lanes((1 - c) * 512, 512)]
    landed(ow_there, sib_rs.at[0])

    group = z * 4 + x
    place16 = lambda g: (y * 4 + g % 4, (g // 4) * 2 + c)

    def attn_copy(g):
        return remote(aout.at[g], ain.at[group], at_ss, at_rs, place16(g))

    for chunk in range(0, 16, CHUNK):
        landed(ctx.at[pl.ds(0, CHUNK - (chunk == 0))], ctx_rs.at[chunk // CHUNK])
        groups = [lax.rem(p + 16 - by, 16) for by in range(chunk, chunk + CHUNK)]
        sums = lax.dot_general(
            jnp.concatenate([ctx[g] for g in groups], axis=0), ow[...], (((1,), (1,)), ((), ())), preferred_element_type=F32
        )
        for i, g in enumerate(groups):
            aout[g] = sums[i * 16 : (i + 1) * 16]
            pl.when(g != group)(attn_copy(g).start)
    gone(aout.at[pl.ds(0, 15)], at_ss)
    ain[group] = aout[group]
    res_receive()
    landed(ain.at[pl.ds(0, 15)], at_rs)
    attn = jnp.concatenate([ain[i] + ain[4 + i] + ain[8 + i] + ain[12 + i] for i in range(4)], axis=1)
    residual = jnp.concatenate([rres[0], rres[1]], axis=1).astype(F32)
    share = lanes(y * SHARE, SHARE)
    post, final = pg[:, share], fg[:, share]

    def y_sum(which, values):
        lane = lax.broadcasted_iota(jnp.int32, (16, 128), 1)
        packed = jnp.zeros((16, 128), F32)
        for i, value in enumerate(values):
            packed = jnp.where(lane == i, jnp.sum(value, axis=1, keepdims=True), packed)
        nbuf[which, y] = packed
        for by in NEAR:
            remote(
                nbuf.at[which, y], nbuf.at[which, y], y_ss.at[which], y_rs.at[which], place(moved(at, "y", by))
            ).start()
        gone(nbuf.at[which, pl.ds(0, 3)], y_ss.at[which])
        landed(nbuf.at[which, pl.ds(0, 3)], y_rs.at[which])
        total = nbuf[which, 0] + nbuf[which, 1] + nbuf[which, 2] + nbuf[which, 3]
        return [total[:, i : i + 1] for i in range(len(values))]

    gained = attn * post
    attn_sq, res_sq, mixed, gained_sq = y_sum(0, [attn * attn, residual * residual, residual * gained, gained * gained])
    inv_attn = lax.rsqrt(attn_sq / WIDTH + epsilon)
    stream = residual + attn * inv_attn * post
    stream_sq = jnp.maximum(res_sq + 2.0 * inv_attn * mixed + inv_attn * inv_attn * gained_sq, 0.0)
    inv_stream = lax.rsqrt(stream_sq / WIDTH + epsilon)
    normed = (stream * inv_stream * final).astype(BF16)
    attn_s[...] = attn
    stream_s[...] = stream
    nbuf[2, 0] = jnp.broadcast_to(inv_attn, (16, 128))
    nbuf[2, 1] = jnp.broadcast_to(inv_stream, (16, 128))

    my_y = lanes(y * 128, 128)
    for q in range(PANELS):
        gath[q, c, z, x, :, my_y] = normed[:, q * 128 : (q + 1) * 128]

    def region(q, here, done):
        return gath.at[
            q,
            here["c"],
            pl.ds(0, 4) if "z" in done else here["z"],
            pl.ds(0, 4) if "x" in done else here["x"],
            :,
            pl.ds(0, 512) if "y" in done else lanes(here["y"] * 128, 128),
        ]

    def ag_start(q, stage):
        dims = GATHER[q % 3]
        src = region(q, at, dims[:stage])
        for by in NEAR:
            remote(src, src, ag_ss.at[stage], ag_rs.at[q, stage], place(moved(at, dims[stage], by))).start()

    def three_regions(q, stage):
        if stage == 0:
            return gath.at[q, c, 0, pl.ds(0, 3), :, pl.ds(0, 128)]
        if stage == 1:
            return gath.at[q, c, pl.ds(0, 3), :, :, pl.ds(0, 128)]
        return gath.at[q, c, pl.ds(0, 3)]

    def ag_wait(q, stage):
        landed(three_regions(q, stage), ag_rs.at[q, stage])

    for q in range(PANELS):
        ag_start(q, 0)
    for stage in (1, 2):
        for q in range(PANELS):
            ag_wait(q, stage - 1)
            ag_start(q, stage)
    pltpu.make_async_copy(wv, wv, w_sem).wait()

    def logits(third, which):
        rows = lambda: rows_of(which * 256, 256)

        @pl.loop(0, 4)
        def _(block):
            cols = lanes(block * 256, 256)
            total = None
            for q in range(third * 3, third * 3 + 3):
                term = jnp.dot(gath[q, which].reshape(256, 512), wv[q, :, cols], preferred_element_type=F32)
                total = term if total is None else total + term
            if third > 0:
                total = total + cap[rows(), cols]
            if third < 2:
                cap[rows(), cols] = total
            else:
                capped = softcap * jnp.tanh(total * (1.0 / softcap))
                cap[rows(), cols] = capped
                expd = jnp.exp(capped)
                first_col = m * 1024 + p * 8192 + block * 256
                ids = lax.broadcasted_iota(jnp.int32, (256, 128), 1) + first_col
                wanted = tgt[rows(), :]
                sums = expd[:, :128] + expd[:, 128:]
                hits = jnp.where(ids == wanted, capped[:, :128], 0.0) + jnp.where(
                    ids + 128 == wanted, capped[:, 128:], 0.0
                )

                @pl.when(block == 0)
                def _():
                    part[rows(), :] = sums
                    hot[rows(), :] = hits

                @pl.when(block > 0)
                def _():
                    part[rows(), :] += sums
                    hot[rows(), :] += hits

    for stage in range(3):
        gone(three_regions(pl.ds(0, PANELS), stage), ag_ss.at[stage])
    for third in range(3):
        panels = pl.ds(third * 3, 3)
        for q in range(third * 3, third * 3 + 3):
            ag_wait(q, 2)
        remote(gath.at[panels, c], gath.at[panels, c], agc_ss, agc_rs.at[third], sib).start()
        logits(third, c)
        landed(gath.at[panels, 1 - c], agc_rs.at[third])
        logits(third, 1 - c)
    gone(gath.at[:, c], agc_ss)

    for i in range(4):
        psrc[i : i + 1, :] = jnp.sum(part[i * 128 : (i + 1) * 128, :].T, axis=0, keepdims=True)
        psrc[i + 4 : i + 5, :] = jnp.sum(hot[i * 128 : (i + 1) * 128, :].T, axis=0, keepdims=True)
    pipe_in[p] = psrc[...]

    def pipe_send(j, _):
        remote(psrc, pipe_in.at[p], tp_ss, tp_rs, (lax.rem(p + j, 16), m)).start()
        return 0

    lax.fori_loop(1, 16, pipe_send, 0)
    gone(pipe_in.at[pl.ds(0, 15)], tp_ss)

    @pl.loop(0, PANELS)
    def _(q):
        turned_q[q] = gath[q].reshape(512, 512).T

    n_copy = pltpu.make_async_copy(turned_q, n_out, out_sem.at[0])
    n_copy.start()
    pending.append(n_copy.wait)
    landed(pipe_in.at[pl.ds(0, 15)], tp_rs)
    mp_in[m] = jnp.sum(pipe_in[...], axis=0)

    def mp_send(j, _):
        remote(mp_in.at[m], mp_in.at[m], tm_ss, tm_rs, (p, lax.rem(m + j, 8))).start()
        return 0

    lax.fori_loop(1, 8, mp_send, 0)
    gone(mp_in.at[pl.ds(0, 7)], tm_ss)
    landed(mp_in.at[pl.ds(0, 7)], tm_rs)
    sums = jnp.sum(mp_in[...], axis=0)
    totals, target_logit = sums[:4], sums[4:]
    loss_out[...] = jnp.sum(
        jnp.sum(jnp.log(totals) - target_logit, axis=0, keepdims=True), axis=1, keepdims=True
    ) * (1.0 / 512)
    inverse = 1.0 / totals
    for i in range(4):
        scale[i * 128 : (i + 1) * 128, :] = jnp.broadcast_to(inverse[i : i + 1, :], (128, 128)).T

    @pl.loop(0, 16)
    def _(block):
        rows = rows_of(block * 32, 32)
        wanted, inv = tgt[rows, :], scale[rows, :]
        ids = lax.broadcasted_iota(jnp.int32, (32, 128), 1) + (m * 1024 + p * 8192)
        for j in range(8):
            cols = slice(j * 128, (j + 1) * 128)
            capped = cap[rows, cols]
            ratio = capped * (1.0 / softcap)
            hit = jnp.where(ids + j * 128 == wanted, 1.0, 0.0)
            grad[rows, cols] = ((jnp.exp(capped) * inv - hit) * (1.0 - ratio * ratio)).astype(BF16)

    g_copy = pltpu.make_async_copy(grad, g_out, out_sem.at[1])
    g_copy.start()
    pending.append(g_copy.wait)

    def grad_dot(q, which):
        rows = rows_of(which * 256, 256)
        return lax.dot_general(grad[rows, :], wv[q], (((1,), (1,)), ((), ())), preferred_element_type=F32).reshape(
            4, 4, 16, 512
        )

    def rs_sib(q):
        sib_out[q] = grad_dot(q, 1 - c).astype(BF16)
        remote(sib_out.at[q], sib_in.at[q], rc_ss, rc_rs.at[q], sib).start()

    def piece(ref, dim, index, left, lead):
        where = list(lead)
        for d in ("z", "x"):
            if d in left:
                where.append(index if d == dim else pl.ds(0, 4))
        where.append(pl.ds(0, 16))
        if "y" in left:
            where.append(lanes(index * 128, 128) if dim == "y" else pl.ds(0, 512))
        else:
            where.append(pl.ds(0, 128))
        return tuple(where)

    r1 = (r1a, r1b, r1c)
    r2 = (r2a, r2b, r2c)
    dims_of = lambda q: GATHER[q % 3][::-1]

    def rs_first(q):
        landed(sib_in.at[q], rc_rs.at[q])
        total = keep[q] + sib_in[q].astype(F32)
        keep[q] = total
        first[q] = total.astype(BF16)
        dim = dims_of(q)[0]
        for by in NEAR:
            there = moved(at, dim, by)
            src = first.at[piece(first, dim, there[dim], ("z", "x", "y"), (q,))]
            remote(src, r1[q % 3].at[q // 3, by - 1], rs_ss.at[q % 3, 0], rs_rs.at[q, 0], place(there)).start()

    def rs_second(q):
        k, r = q % 3, q // 3
        got = r1[k].at[r]
        landed(got, rs_rs.at[q, 0])
        dims = dims_of(q)
        left = [d for d in ("z", "x", "y") if d != dims[0]]
        total = keep[piece(keep, dims[0], at[dims[0]], ("z", "x", "y"), (q,))]
        total = total + got[0].astype(F32) + got[1].astype(F32) + got[2].astype(F32)
        own2[k][r] = total
        s2[k][r] = total.astype(BF16)
        for by in NEAR:
            there = moved(at, dims[1], by)
            src = s2[k].at[piece(s2[k], dims[1], there[dims[1]], left, (r,))]
            remote(src, r2[k].at[r, by - 1], rs_ss.at[q % 3, 1], rs_rs.at[q, 1], place(there)).start()

    def rs_third(q):
        k, r = q % 3, q // 3
        got = r2[k].at[r]
        landed(got, rs_rs.at[q, 1])
        dims = dims_of(q)
        left = [d for d in ("z", "x", "y") if d != dims[0]]
        total = own2[k][piece(own2[k], dims[1], at[dims[1]], left, (r,))]
        total = total + got[0].astype(F32) + got[1].astype(F32) + got[2].astype(F32)
        s3[k][r] = total
        for by in NEAR:
            there = moved(at, dims[2], by)
            src = s3[k].at[piece(s3[k], dims[2], there[dims[2]], [dims[2]], (r,))]
            remote(src, r3.at[q, by - 1], rs_ss.at[q % 3, 2], rs_rs.at[q, 2], place(there)).start()

    def rs_last(q):
        k, r = q % 3, q // 3
        landed(r3.at[q], rs_rs.at[q, 2])
        dims = dims_of(q)
        own = s3[k][piece(s3[k], dims[2], at[dims[2]], [dims[2]], (r,))]
        gsum[:, q * 128 : (q + 1) * 128] = own + r3[q, 0] + r3[q, 1] + r3[q, 2]

    def head_early(q):
        early[q] = jnp.dot(turned_q[q], grad[...], preferred_element_type=F32).astype(BF16).reshape(4, 128, 1024)
        copy = pltpu.make_async_copy(early.at[q], x_out.at[q], early_sem.at[q])
        copy.start()
        pending.append(copy.wait)

    rs_sib(0)
    for q in range(PANELS):
        keep[q] = grad_dot(q, c)
        if q + 1 < PANELS:
            rs_sib(q + 1)
        rs_first(q)
    for q in range(PANELS):
        if q % 2 == 0 and q // 2 < EARLY:
            head_early(q // 2)
        rs_second(q)
    for q in range(PANELS):
        rs_third(q)
    for q in range(PANELS):
        rs_last(q)
    gone(sib_out, rc_ss)
    for k in range(3):
        gone(r1[k], rs_ss.at[k, 0])
        gone(r2[k], rs_ss.at[k, 1])
        gone(r3.at[pl.ds(0, 3)], rs_ss.at[k, 2])

    stream, attn = stream_s[...], attn_s[...]
    inv_attn, inv_stream = nbuf[2, 0][:, :1], nbuf[2, 1][:, :1]
    post, final = pg[:, share], fg[:, share]
    upstream = gsum[...] * final
    gained = attn * post
    cross, cross_up, cross_stream = y_sum(1, [stream * upstream, gained * upstream, gained * stream])
    factor = inv_stream * inv_stream * (cross / WIDTH)
    grad_stream = inv_stream * (upstream - stream * factor)
    cross_attn = inv_stream * (cross_up - factor * cross_stream)
    grad_attn = (inv_attn * (grad_stream * post - attn * (inv_attn * inv_attn) * (cross_attn / WIDTH))).astype(BF16)
    for i in range(4):
        gout[i] = grad_attn[:, i * COLS : (i + 1) * COLS]

    def ga_send(j, _):
        g = lax.rem(group + j, 16)
        remote(gout.at[g % 4], gin.at[group], ga_ss, ga_rs, place16(g)).start()
        return 0

    lax.fori_loop(1, 16, ga_send, 0)
    gone(gin.at[pl.ds(0, 15)], ga_ss)
    gin[group] = gout[x]
    d_res = grad_stream.astype(BF16)
    dsend[0] = d_res[:, :576]
    dsend[1] = d_res[:, 576:]
    dres_receive = turn([dsend.at[0], dsend.at[1]], drecv, 1)
    landed(gin.at[pl.ds(0, 15)], ga_rs)
    ga = gin[...].reshape(256, COLS)
    dcs[...] = jnp.dot(ga, ow[...], preferred_element_type=F32).astype(BF16).reshape(16, 16, 1024)

    def dc_send(j, _):
        i = peer32(j)
        remote(
            dcs.at[i // 2, :, lanes((i % 2) * 512, 512)], dcr.at[me], dc_ss, dc_rs, place32(i)
        ).start()
        return 0

    lax.fori_loop(1, 32, dc_send, 0)
    dcr[me] = dcs[p, :, my_lanes]

    def og_dot(which):
        heads = ctx[:, :, lanes(which * 512, 512)].reshape(256, 512)
        return lax.dot_general(ga, heads, (((0,), (0,)), ((), ())), preferred_element_type=F32)

    ogs[...] = og_dot(1 - c)
    og_copy = remote(ogs, ogr, sib_ss.at[1], sib_rs.at[1], sib)
    og_copy.start()
    og_own = og_dot(c)
    og_copy.wait_recv()
    og_out[...] = (og_own + ogr[...]).astype(BF16)
    dres_receive()
    for cc in range(2):
        dres_out[cc * 16 : (cc + 1) * 16, :] = drecv[cc]

    finish()
    og_copy.wait_send()

    landed(dcr.at[pl.ds(0, 31)], dc_rs)
    remote(dcr.at[pl.ds(0, 31)], dcr.at[pl.ds(0, 31)], dc_ss, dc_rs, sib).wait_send()
    for cc in range(2):
        total = dcr[cc].astype(F32)
        for i in range(1, 16):
            total = total + dcr[2 * i + cc].astype(F32)
        dctx_out[cc * 16 : (cc + 1) * 16, :] = total.astype(BF16)


def section_listed(*refs):
    ins, outs, rest = refs[:7], refs[7:14], refs[14:]
    names, n = [], 0
    for count in LAYOUT:
        names.append(rest[n] if count == 1 else tuple(rest[n : n + count]))
        n += count
    section(*ins, *outs, *names)


VM = pltpu.VMEM
DMA = pltpu.SemaphoreType.DMA
SCRATCH = [
    VM((9, 512, 1024), BF16),
    VM((16, 16, 1024), BF16),
    VM((COLS, 1024), BF16),
    VM((1, WIDTH), F32),
    VM((1, WIDTH), F32),
    VM((2, 16, 576), BF16),
    VM((16, 16, COLS), F32),
    VM((16, 16, COLS), F32),
    VM((16, SHARE), F32),
    VM((16, SHARE), F32),
    VM((3, 4, 16, 128), F32),
    VM((9, 2, 4, 4, 16, 512), BF16),
    VM((9, 512, 512), BF16),
    VM((512, 1024), F32),
    VM((512, 128), jnp.int32),
    VM((512, 128), F32),
    VM((512, 128), F32),
    VM((8, 128), F32),
    VM((16, 8, 128), F32),
    VM((8, 8, 128), F32),
    VM((512, 128), F32),
    VM((512, 1024), BF16),
    VM((EARLY, 4, 128, 1024), BF16),
    VM((9, 4, 4, 16, 512), F32),
    VM((9, 4, 4, 16, 512), BF16),
    VM((9, 4, 4, 16, 512), BF16),
    VM((9, 4, 4, 16, 512), BF16),
    VM((3, 3, 4, 16, 512), BF16),
    VM((3, 3, 4, 4, 16, 128), BF16),
    VM((3, 3, 4, 16, 512), BF16),
    (VM((3, 4, 16, 512), BF16), VM((3, 4, 4, 16, 128), BF16), VM((3, 4, 16, 512), BF16)),
    (VM((3, 4, 16, 512), F32), VM((3, 4, 4, 16, 128), F32), VM((3, 4, 16, 512), F32)),
    VM((3, 3, 16, 512), BF16),
    VM((3, 3, 4, 16, 128), BF16),
    VM((3, 3, 4, 16, 128), BF16),
    (VM((3, 16, 512), F32), VM((3, 4, 16, 128), F32), VM((3, 4, 16, 128), F32)),
    VM((9, 3, 16, 128), F32),
    VM((16, SHARE), F32),
    VM((4, 16, COLS), BF16),
    VM((16, 16, COLS), BF16),
    VM((16, 16, 1024), BF16),
    VM((32, 16, 512), BF16),
    VM((COLS, 512), F32),
    VM((COLS, 512), F32),
    VM((2, 16, 576), BF16),
    VM((2, 16, 576), BF16),
    DMA,
    DMA((1,)), DMA((16 // CHUNK,)),
    DMA((3,)), DMA((3,)),
    DMA((2, 2)), DMA((2, 2)),
    DMA, DMA,
    DMA((2,)), DMA((2,)),
    DMA((3,)), DMA((9, 3)),
    DMA, DMA((3,)),
    DMA, DMA,
    DMA, DMA,
    DMA, DMA((9,)),
    DMA((3, 3)), DMA((9, 3)),
    DMA, DMA,
    DMA, DMA,
    DMA((2,)),
    DMA((EARLY,)),
]
LAYOUT = [len(s) if type(s) is tuple else 1 for s in SCRATCH]
FLAT = [t for s in SCRATCH for t in (s if type(s) is tuple else (s,))]


def head_grad_kernel(
    n_hbm, g_hbm, x_hbm, loss_in, og_in, dres_in, dctx_in, hg_hbm, loss_ref, og_out, dres_out, dctx_out,
    n_buf, g_buf, x_buf, out_buf, og_buf, dres_buf, dctx_buf, n_sem, g_sem, x_sem, out_sem, small_sem,
):
    panels = range(EARLY, PANELS)
    g_copy = pltpu.make_async_copy(g_hbm, g_buf, g_sem)
    n_copies = {q: pltpu.make_async_copy(n_hbm.at[q], n_buf.at[q - EARLY], n_sem.at[q - EARLY]) for q in panels}
    x_copies = [pltpu.make_async_copy(x_hbm.at[q], x_buf.at[q], x_sem.at[q]) for q in range(EARLY)]
    small = ((og_in, og_buf, og_out), (dres_in, dres_buf, dres_out), (dctx_in, dctx_buf, dctx_out))
    small_in = [pltpu.make_async_copy(a, b, small_sem.at[0, i]) for i, (a, b, _) in enumerate(small)]
    small_out = [pltpu.make_async_copy(b, a, small_sem.at[1, i]) for i, (_, b, a) in enumerate(small)]
    g_copy.start()
    for i, q in enumerate(panels):
        n_copies[q].start()
        if i < EARLY:
            x_copies[i].start()
    for copy in small_in:
        copy.start()
    loss_ref[...] = loss_in[...]
    g_copy.wait()
    outs = []

    def write(source, q):
        copy = pltpu.make_async_copy(source, hg_hbm.at[:, q], out_sem.at[q])
        copy.start()
        outs.append(copy)

    for i, q in enumerate(panels):
        n_copies[q].wait()
        product = jnp.dot(n_buf[i], g_buf[...], preferred_element_type=F32)
        out_buf[i] = product.astype(BF16).reshape(4, 128, 1024)
        write(out_buf.at[i], q)
        if i < EARLY:
            x_copies[i].wait()
            write(x_buf.at[i], i)
    for one, two in zip(small_in, small_out):
        one.wait()
        two.start()
    for copy in outs + small_out:
        copy.wait()


def on_device(context, residual_in, o_weight, post_gain, final_gain, head_weight, targets):
    vmem, hbm = pl.BlockSpec(memory_space=pltpu.VMEM), pl.BlockSpec(memory_space=pl.ANY)
    shape = jax.ShapeDtypeStruct
    small = [shape((1, 1), F32), shape((COLS, 512), BF16), shape((32, 576), BF16), shape((32, 512), BF16)]
    normed, grad, early, loss, og, dres, dctx = pl.pallas_call(
        section_listed,
        out_shape=[shape((9, 512, 512), BF16), shape((512, 1024), BF16), shape((EARLY, 4, 128, 1024), BF16), *small],
        in_specs=[vmem, vmem, vmem, vmem, vmem, hbm, vmem],
        out_specs=[hbm, hbm, hbm, vmem, vmem, vmem, vmem],
        scratch_shapes=FLAT,
        compiler_params=pltpu.CompilerParams(
            collective_id=0, has_side_effects=True, vmem_limit_bytes=60 * 2**20
        ),
        cost_estimate=pl.CostEstimate(flops=10**10, bytes_accessed=20 * 10**6, transcendentals=10**6),
        name="section",
    )(
        context,
        residual_in,
        o_weight.T,
        post_gain,
        final_gain,
        head_weight.reshape(4, 9, 128, 1024),
        targets.reshape(4, 128),
    )
    rest = PANELS - EARLY
    head_grad, loss, og, dres, dctx = pl.pallas_call(
        head_grad_kernel,
        out_shape=[shape((4, 9, 128, 1024), BF16), *small],
        in_specs=[hbm, hbm, hbm, vmem, hbm, hbm, hbm],
        out_specs=[hbm, vmem, hbm, hbm, hbm],
        scratch_shapes=[
            VM((rest, 512, 512), BF16), VM((512, 1024), BF16), VM((EARLY, 4, 128, 1024), BF16),
            VM((rest, 4, 128, 1024), BF16), VM((COLS, 512), BF16), VM((32, 576), BF16), VM((32, 512), BF16),
            DMA((rest,)), DMA, DMA((EARLY,)), DMA((PANELS,)), DMA((2, 3)),
        ],
        compiler_params=pltpu.CompilerParams(vmem_limit_bytes=60 * 2**20),
        cost_estimate=pl.CostEstimate(flops=3 * 10**9, bytes_accessed=18 * 10**6, transcendentals=0),
        name="head_grad",
    )(normed, grad, early, loss, og, dres, dctx)
    return (loss.reshape(()), head_grad.reshape(WIDTH, 1024), og.T, dres, dctx)


def solution(mesh):
    placed = (
        P("pipe", "mp"),
        P("pipe", "mp"),
        P("mp", "pipe"),
        P(),
        P(),
        P(None, ("pipe", "mp")),
        P(),
    )
    return jax.shard_map(
        on_device,
        mesh=mesh,
        in_specs=placed,
        out_specs=(P(), P(None, ("pipe", "mp")), P("mp", "pipe"), P("pipe", "mp"), P("pipe", "mp")),
        check_vma=False,
    )
```

time: 148 us -> 116 us (0.78)
  Pallas kernels: 137 us -> 115 us
  local copies, waits for them, and re-layouts: 9.2 us -> 0 us
    pallas_call x2, Pallas kernels: 137 us -> 115 us  [the longest x1 106 us: on_device(): pl.pallas_call(section_listed, out_shape=[shape((9, 512, 512), BF16), sha...]
    unnamed x10 -> x0, local copies, waits for them, and re-layouts: 6.51 us -> none
    reshape x2 -> x0, local copies, waits for them, and re-layouts: 2.69 us -> none  [the longest x1 1.35 us: on_device(): post_gain.reshape(1, WIDTH)]
where the time goes in v2:
time: 116 us
  Pallas kernels  115 us (99%)
    pallas_call x1, Pallas kernels, on_device(): pl.pallas_call(section_listed, out_shape=[shape((9, 512, 512), BF16), sha...  106 us
    pallas_call x1, Pallas kernels, on_device(): pl.pallas_call(head_grad_kernel, out_shape=[shape((4, 9, 128, 1024), BF16...  8.82 us

profile of v2, /device:TPU:1, one launch (start us, length us, event | category | flops | bytes accessed | tf_op | source)
XLA Modules:
  0.0 115.7 jit_solution(2972555805665111617)
XLA Ops:
  0.6 106.0 %section.1 = (bf16[9,512,512]{2,1,0:T(8,128)(2,1)}, bf16[512,1024]{1,0:T(8,128)(2,1)}, bf16[4,4,128,1024]{3,2,1,0:T(8,128)(2,1)}, f32[1,1]{1,0:T(1,128)}, bf16[2...) custom-call(bf16[32,512]{1,0:T(8,128)(2,1)} %refs_0_.1, bf16[32,576]{1,0:T(8,128)(2,1)} %refs_1_.1, ...), custom_call_target="tpu_custom_call" | custom-call | flops 10000000000 | bytes 20000000 | tf_op jit(solution)/shard_map/section/pallas_call | solution.py:652
  106.7 8.8 %head_grad.1 = (bf16[4,9,128,1024]{3,2,1,0:T(8,128)(2,1)}, f32[1,1]{1,0:T(1,128)}, bf16[288,512]{1,0:T(8,128)(2,1)}, bf16[32,576]{1,0:T(8,128)(2,1)}, bf16[32,512]{1,0:T(8,128)(2,1)}) custom-call(bf16[9,512,512]{2,1,0:T(8,128)(2,1)} %get-tuple-element.17.n_hbm, bf16[512,1024]{1,0:T(8,128)(2,1)} %get-tuple-element.18.g_hbm, ...), custom_call_target="tpu_custom_call" | custom-call | flops 3000000000 | bytes 18000000 | tf_op jit(solution)/shard_map/head_grad/pallas_call | solution.py:673

commit v3 on v2

--- a/solution.py
+++ b/solution.py
@@ -14,7 +14,6 @@
 SHARE = 1152
 PANELS = 9
 CHUNK = 8
-EARLY = 4
 COLS = 288
 GATHER = (("y", "x", "z"), ("x", "z", "y"), ("z", "y", "x"))
 NEAR = (1, 3, 2)
@@ -45,13 +44,13 @@
 
 def section(
     ctx_ref, res_ref, ow_ref, pg_ref, fg_ref, w_hbm, tgt_ref,
-    n_out, g_out, x_out, loss_out, og_out, dres_out, dctx_out,
+    x_out, loss_out, og_out, dres_out, dctx_out,
     wv, ctx, ow, pg, fg, rres, aout, ain, attn_s, stream_s, nbuf, gath, turned_q, cap, tgt, hot, part,
-    psrc, pipe_in, mp_in, scale, grad, early,
+    psrc, pipe_in, mp_in, scale, aim, grad,
     keep, sib_out, sib_in, first, r1a, r1b, r1c, s2, own2, r2a, r2b, r2c, s3, r3,
     gsum, gout, gin, dcs, dcr, ogs, ogr, dsend, drecv,
     w_sem, ctx_ss, ctx_rs, sib_ss, sib_rs, tn_ss, tn_rs, at_ss, at_rs, y_ss, y_rs, ag_ss, ag_rs, agc_ss, agc_rs, tp_ss, tp_rs, tm_ss, tm_rs,
-    rc_ss, rc_rs, rs_ss, rs_rs, ga_ss, ga_rs, dc_ss, dc_rs, out_sem, early_sem,
+    rc_ss, rc_rs, rs_ss, rs_rs, ga_ss, ga_rs, dc_ss, dc_rs,
 ):
     p, m = lax.axis_index("pipe"), lax.axis_index("mp")
     y, x, z, c = p // 4, p % 4, m // 2, m % 2
@@ -238,7 +237,7 @@
         dims = GATHER[q % 3]
         src = region(q, at, dims[:stage])
         for by in NEAR:
-            remote(src, src, ag_ss.at[stage], ag_rs.at[q, stage], place(moved(at, dims[stage], by))).start()
+            remote(src, src, ag_ss.at[stage if stage < 2 else 2 + q // 3], ag_rs.at[q, stage], place(moved(at, dims[stage], by))).start()
 
     def three_regions(q, stage):
         if stage == 0:
@@ -252,58 +251,83 @@
 
     for q in range(PANELS):
         ag_start(q, 0)
-    for stage in (1, 2):
-        for q in range(PANELS):
-            ag_wait(q, stage - 1)
-            ag_start(q, stage)
+    for q in range(PANELS):
+        ag_wait(q, 0)
+        ag_start(q, 1)
+
+    def ag_last(third):
+        for q in range(third * 3, third * 3 + 3):
+            ag_wait(q, 1)
+            ag_start(q, 2)
+
+    def ag_sent(third):
+        regions = three_regions(pl.ds(third * 3, 3), 2)
+        remote(regions, regions, ag_ss.at[2 + third], ag_ss.at[2 + third], sib).wait_send()
+
+    ag_last(0)
     pltpu.make_async_copy(wv, wv, w_sem).wait()
 
     def logits(third, which):
-        rows = lambda: rows_of(which * 256, 256)
-
-        @pl.loop(0, 4)
-        def _(block):
-            cols = lanes(block * 256, 256)
+        rows = rows_of(which * 256, 256)
+
+        def product(cols):
             total = None
             for q in range(third * 3, third * 3 + 3):
                 term = jnp.dot(gath[q, which].reshape(256, 512), wv[q, :, cols], preferred_element_type=F32)
                 total = term if total is None else total + term
-            if third > 0:
-                total = total + cap[rows(), cols]
-            if third < 2:
-                cap[rows(), cols] = total
-            else:
-                capped = softcap * jnp.tanh(total * (1.0 / softcap))
-                cap[rows(), cols] = capped
-                expd = jnp.exp(capped)
-                first_col = m * 1024 + p * 8192 + block * 256
-                ids = lax.broadcasted_iota(jnp.int32, (256, 128), 1) + first_col
-                wanted = tgt[rows(), :]
-                sums = expd[:, :128] + expd[:, 128:]
-                hits = jnp.where(ids == wanted, capped[:, :128], 0.0) + jnp.where(
-                    ids + 128 == wanted, capped[:, 128:], 0.0
-                )
-
-                @pl.when(block == 0)
-                def _():
-                    part[rows(), :] = sums
-                    hot[rows(), :] = hits
-
-                @pl.when(block > 0)
-                def _():
-                    part[rows(), :] += sums
-                    hot[rows(), :] += hits
-
-    for stage in range(3):
+            return total
+
+        if third == 0:
+            for n in range(0, 1024, 512):
+                cap[rows, n : n + 512] = product(slice(n, n + 512))
+        elif third == 1:
+            for n in range(0, 1024, 512):
+                cap[rows, n : n + 512] += product(slice(n, n + 512))
+        else:
+            sums = hits = None
+            wanted = tgt[rows, :]
+            ids = lax.broadcasted_iota(jnp.int32, (256, 128), 1) + (m * 1024 + p * 8192)
+            for n in range(0, 1024, 256):
+                total = product(slice(n, n + 256)) + cap[rows, n : n + 256]
+                for i in range(0, 256, 128):
+                    capped = softcap * jnp.tanh(total[:, i : i + 128] * (1.0 / softcap))
+                    cap[rows, n + i : n + i + 128] = capped
+                    expd = jnp.exp(capped)
+                    hit = jnp.where(ids + (n + i) == wanted, capped, 0.0)
+                    sums = expd if sums is None else sums + expd
+                    hits = hit if hits is None else hits + hit
+            part[rows, :] = sums
+            hot[rows, :] = hits
+
+    for stage in range(2):
         gone(three_regions(pl.ds(0, PANELS), stage), ag_ss.at[stage])
-    for third in range(3):
+
+    def ag_arrived(third):
         panels = pl.ds(third * 3, 3)
         for q in range(third * 3, third * 3 + 3):
             ag_wait(q, 2)
         remote(gath.at[panels, c], gath.at[panels, c], agc_ss, agc_rs.at[third], sib).start()
-        logits(third, c)
-        landed(gath.at[panels, 1 - c], agc_rs.at[third])
-        logits(third, 1 - c)
+
+    def ag_other(third):
+        landed(gath.at[pl.ds(third * 3, 3), 1 - c], agc_rs.at[third])
+
+    ag_sent(0)
+    ag_last(1)
+    ag_arrived(0)
+    logits(0, c)
+    ag_sent(1)
+    ag_last(2)
+    ag_other(0)
+    logits(0, 1 - c)
+    ag_arrived(1)
+    logits(1, c)
+    ag_other(1)
+    logits(1, 1 - c)
+    ag_sent(2)
+    ag_arrived(2)
+    logits(2, c)
+    ag_other(2)
+    logits(2, 1 - c)
     gone(gath.at[:, c], agc_ss)
 
     for i in range(4):
@@ -322,9 +346,6 @@
     def _(q):
         turned_q[q] = gath[q].reshape(512, 512).T
 
-    n_copy = pltpu.make_async_copy(turned_q, n_out, out_sem.at[0])
-    n_copy.start()
-    pending.append(n_copy.wait)
     landed(pipe_in.at[pl.ds(0, 15)], tp_rs)
     mp_in[m] = jnp.sum(pipe_in[...], axis=0)
 
@@ -334,6 +355,20 @@
 
     lax.fori_loop(1, 8, mp_send, 0)
     gone(mp_in.at[pl.ds(0, 7)], tm_ss)
+
+    @pl.loop(0, 16)
+    def _(block):
+        rows = rows_of(block * 32, 32)
+        wanted = tgt[rows, :]
+        ids = lax.broadcasted_iota(jnp.int32, (32, 128), 1) + (m * 1024 + p * 8192)
+        for j in range(8):
+            cols = slice(j * 128, (j + 1) * 128)
+            capped = cap[rows, cols]
+            ratio = capped * (1.0 / softcap)
+            slope = 1.0 - ratio * ratio
+            cap[rows, cols] = jnp.exp(capped) * slope
+            aim[rows, cols] = jnp.where(ids + j * 128 == wanted, slope, 0.0)
+
     landed(mp_in.at[pl.ds(0, 7)], tm_rs)
     sums = jnp.sum(mp_in[...], axis=0)
     totals, target_logit = sums[:4], sums[4:]
@@ -344,21 +379,14 @@
     for i in range(4):
         scale[i * 128 : (i + 1) * 128, :] = jnp.broadcast_to(inverse[i : i + 1, :], (128, 128)).T
 
-    @pl.loop(0, 16)
-    def _(block):
-        rows = rows_of(block * 32, 32)
-        wanted, inv = tgt[rows, :], scale[rows, :]
-        ids = lax.broadcasted_iota(jnp.int32, (32, 128), 1) + (m * 1024 + p * 8192)
-        for j in range(8):
-            cols = slice(j * 128, (j + 1) * 128)
-            capped = cap[rows, cols]
-            ratio = capped * (1.0 / softcap)
-            hit = jnp.where(ids + j * 128 == wanted, 1.0, 0.0)
-            grad[rows, cols] = ((jnp.exp(capped) * inv - hit) * (1.0 - ratio * ratio)).astype(BF16)
-
-    g_copy = pltpu.make_async_copy(grad, g_out, out_sem.at[1])
-    g_copy.start()
-    pending.append(g_copy.wait)
+    def logit_grad(which):
+        @pl.loop(0, 4)
+        def _(block):
+            rows = rows_of(which * 256 + block * 64, 64)
+            inv = scale[rows, :]
+            for j in range(8):
+                cols = slice(j * 128, (j + 1) * 128)
+                grad[rows, cols] = (cap[rows, cols] * inv - aim[rows, cols]).astype(BF16)
 
     def grad_dot(q, which):
         rows = rows_of(which * 256, 256)
@@ -388,9 +416,7 @@
 
     def rs_first(q):
         landed(sib_in.at[q], rc_rs.at[q])
-        total = keep[q] + sib_in[q].astype(F32)
-        keep[q] = total
-        first[q] = total.astype(BF16)
+        first[q] = (keep[q] + sib_in[q].astype(F32)).astype(BF16)
         dim = dims_of(q)[0]
         for by in NEAR:
             there = moved(at, dim, by)
@@ -403,7 +429,8 @@
         landed(got, rs_rs.at[q, 0])
         dims = dims_of(q)
         left = [d for d in ("z", "x", "y") if d != dims[0]]
-        total = keep[piece(keep, dims[0], at[dims[0]], ("z", "x", "y"), (q,))]
+        own = piece(keep, dims[0], at[dims[0]], ("z", "x", "y"), (q,))
+        total = keep[own] + sib_in[own].astype(F32)
         total = total + got[0].astype(F32) + got[1].astype(F32) + got[2].astype(F32)
         own2[k][r] = total
         s2[k][r] = total.astype(BF16)
@@ -434,23 +461,26 @@
         gsum[:, q * 128 : (q + 1) * 128] = own + r3[q, 0] + r3[q, 1] + r3[q, 2]
 
     def head_early(q):
-        early[q] = jnp.dot(turned_q[q], grad[...], preferred_element_type=F32).astype(BF16).reshape(4, 128, 1024)
-        copy = pltpu.make_async_copy(early.at[q], x_out.at[q], early_sem.at[q])
-        copy.start()
-        pending.append(copy.wait)
-
+        x_out[q] = jnp.dot(turned_q[q], grad[...], preferred_element_type=F32).astype(BF16).reshape(4, 128, 1024)
+
+    logit_grad(1 - c)
     rs_sib(0)
+    logit_grad(c)
+    rs_sib(1)
     for q in range(PANELS):
         keep[q] = grad_dot(q, c)
-        if q + 1 < PANELS:
-            rs_sib(q + 1)
+        if q + 2 < PANELS:
+            rs_sib(q + 2)
         rs_first(q)
+    head_early(0)
     for q in range(PANELS):
-        if q % 2 == 0 and q // 2 < EARLY:
-            head_early(q // 2)
         rs_second(q)
+    for q in (1, 2, 3):
+        head_early(q)
     for q in range(PANELS):
         rs_third(q)
+    for q in (4, 5):
+        head_early(q)
     for q in range(PANELS):
         rs_last(q)
     gone(sib_out, rc_ss)
@@ -484,6 +514,8 @@
     dsend[0] = d_res[:, :576]
     dsend[1] = d_res[:, 576:]
     dres_receive = turn([dsend.at[0], dsend.at[1]], drecv, 1)
+    for q in (6, 7):
+        head_early(q)
     landed(gin.at[pl.ds(0, 15)], ga_rs)
     ga = gin[...].reshape(256, COLS)
     dcs[...] = jnp.dot(ga, ow[...], preferred_element_type=F32).astype(BF16).reshape(16, 16, 1024)
@@ -508,6 +540,7 @@
     og_own = og_dot(c)
     og_copy.wait_recv()
     og_out[...] = (og_own + ogr[...]).astype(BF16)
+    head_early(8)
     dres_receive()
     for cc in range(2):
         dres_out[cc * 16 : (cc + 1) * 16, :] = drecv[cc]
@@ -525,7 +558,7 @@
 
 
 def section_listed(*refs):
-    ins, outs, rest = refs[:7], refs[7:14], refs[14:]
+    ins, outs, rest = refs[:7], refs[7:12], refs[12:]
     names, n = [], 0
     for count in LAYOUT:
         names.append(rest[n] if count == 1 else tuple(rest[n : n + count]))
@@ -557,8 +590,8 @@
     VM((16, 8, 128), F32),
     VM((8, 8, 128), F32),
     VM((512, 128), F32),
+    VM((512, 1024), F32),
     VM((512, 1024), BF16),
-    VM((EARLY, 4, 128, 1024), BF16),
     VM((9, 4, 4, 16, 512), F32),
     VM((9, 4, 4, 16, 512), BF16),
     VM((9, 4, 4, 16, 512), BF16),
@@ -588,7 +621,7 @@
     DMA((2, 2)), DMA((2, 2)),
     DMA, DMA,
     DMA((2,)), DMA((2,)),
-    DMA((3,)), DMA((9, 3)),
+    DMA((5,)), DMA((9, 3)),
     DMA, DMA((3,)),
     DMA, DMA,
     DMA, DMA,
@@ -596,52 +629,21 @@
     DMA((3, 3)), DMA((9, 3)),
     DMA, DMA,
     DMA, DMA,
-    DMA((2,)),
-    DMA((EARLY,)),
 ]
 LAYOUT = [len(s) if type(s) is tuple else 1 for s in SCRATCH]
 FLAT = [t for s in SCRATCH for t in (s if type(s) is tuple else (s,))]
 
 
-def head_grad_kernel(
-    n_hbm, g_hbm, x_hbm, loss_in, og_in, dres_in, dctx_in, hg_hbm, loss_ref, og_out, dres_out, dctx_out,
-    n_buf, g_buf, x_buf, out_buf, og_buf, dres_buf, dctx_buf, n_sem, g_sem, x_sem, out_sem, small_sem,
+def hand_over_kernel(
+    x_any, loss_in, og_in, dres_in, dctx_in, hg_hbm, loss_ref, og_out, dres_out, dctx_out, out_sem, small_sem
 ):
-    panels = range(EARLY, PANELS)
-    g_copy = pltpu.make_async_copy(g_hbm, g_buf, g_sem)
-    n_copies = {q: pltpu.make_async_copy(n_hbm.at[q], n_buf.at[q - EARLY], n_sem.at[q - EARLY]) for q in panels}
-    x_copies = [pltpu.make_async_copy(x_hbm.at[q], x_buf.at[q], x_sem.at[q]) for q in range(EARLY)]
-    small = ((og_in, og_buf, og_out), (dres_in, dres_buf, dres_out), (dctx_in, dctx_buf, dctx_out))
-    small_in = [pltpu.make_async_copy(a, b, small_sem.at[0, i]) for i, (a, b, _) in enumerate(small)]
-    small_out = [pltpu.make_async_copy(b, a, small_sem.at[1, i]) for i, (_, b, a) in enumerate(small)]
-    g_copy.start()
-    for i, q in enumerate(panels):
-        n_copies[q].start()
-        if i < EARLY:
-            x_copies[i].start()
-    for copy in small_in:
+    outs = [pltpu.make_async_copy(x_any.at[q], hg_hbm.at[:, q], out_sem.at[q]) for q in range(PANELS)]
+    small = ((og_in, og_out), (dres_in, dres_out), (dctx_in, dctx_out))
+    outs += [pltpu.make_async_copy(a, b, small_sem.at[i]) for i, (a, b) in enumerate(small)]
+    for copy in outs:
         copy.start()
     loss_ref[...] = loss_in[...]
-    g_copy.wait()
-    outs = []
-
-    def write(source, q):
-        copy = pltpu.make_async_copy(source, hg_hbm.at[:, q], out_sem.at[q])
-        copy.start()
-        outs.append(copy)
-
-    for i, q in enumerate(panels):
-        n_copies[q].wait()
-        product = jnp.dot(n_buf[i], g_buf[...], preferred_element_type=F32)
-        out_buf[i] = product.astype(BF16).reshape(4, 128, 1024)
-        write(out_buf.at[i], q)
-        if i < EARLY:
-            x_copies[i].wait()
-            write(x_buf.at[i], i)
-    for one, two in zip(small_in, small_out):
-        one.wait()
-        two.start()
-    for copy in outs + small_out:
+    for copy in outs:
         copy.wait()
 
 
@@ -649,14 +651,14 @@
     vmem, hbm = pl.BlockSpec(memory_space=pltpu.VMEM), pl.BlockSpec(memory_space=pl.ANY)
     shape = jax.ShapeDtypeStruct
     small = [shape((1, 1), F32), shape((COLS, 512), BF16), shape((32, 576), BF16), shape((32, 512), BF16)]
-    normed, grad, early, loss, og, dres, dctx = pl.pallas_call(
+    early, loss, og, dres, dctx = pl.pallas_call(
         section_listed,
-        out_shape=[shape((9, 512, 512), BF16), shape((512, 1024), BF16), shape((EARLY, 4, 128, 1024), BF16), *small],
+        out_shape=[VM(a.shape, a.dtype) for a in (shape((9, 4, 128, 1024), BF16), *small)],
         in_specs=[vmem, vmem, vmem, vmem, vmem, hbm, vmem],
-        out_specs=[hbm, hbm, hbm, vmem, vmem, vmem, vmem],
+        out_specs=[vmem, vmem, vmem, vmem, vmem],
         scratch_shapes=FLAT,
         compiler_params=pltpu.CompilerParams(
-            collective_id=0, has_side_effects=True, vmem_limit_bytes=60 * 2**20
+            collective_id=0, has_side_effects=True, vmem_limit_bytes=46 * 2**20
         ),
         cost_estimate=pl.CostEstimate(flops=10**10, bytes_accessed=20 * 10**6, transcendentals=10**6),
         name="section",
@@ -669,21 +671,16 @@
         head_weight.reshape(4, 9, 128, 1024),
         targets.reshape(4, 128),
     )
-    rest = PANELS - EARLY
     head_grad, loss, og, dres, dctx = pl.pallas_call(
-        head_grad_kernel,
+        hand_over_kernel,
         out_shape=[shape((4, 9, 128, 1024), BF16), *small],
-        in_specs=[hbm, hbm, hbm, vmem, hbm, hbm, hbm],
+        in_specs=[vmem, vmem, vmem, vmem, vmem],
         out_specs=[hbm, vmem, hbm, hbm, hbm],
-        scratch_shapes=[
-            VM((rest, 512, 512), BF16), VM((512, 1024), BF16), VM((EARLY, 4, 128, 1024), BF16),
-            VM((rest, 4, 128, 1024), BF16), VM((COLS, 512), BF16), VM((32, 576), BF16), VM((32, 512), BF16),
-            DMA((rest,)), DMA, DMA((EARLY,)), DMA((PANELS,)), DMA((2, 3)),
-        ],
-        compiler_params=pltpu.CompilerParams(vmem_limit_bytes=60 * 2**20),
-        cost_estimate=pl.CostEstimate(flops=3 * 10**9, bytes_accessed=18 * 10**6, transcendentals=0),
-        name="head_grad",
-    )(normed, grad, early, loss, og, dres, dctx)
+        scratch_shapes=[DMA((PANELS,)), DMA((3,))],
+        compiler_params=pltpu.CompilerParams(vmem_limit_bytes=16 * 2**20),
+        cost_estimate=pl.CostEstimate(flops=0, bytes_accessed=20 * 10**6, transcendentals=0),
+        name="hand_over",
+    )(early, loss, og, dres, dctx)
     return (loss.reshape(()), head_grad.reshape(WIDTH, 1024), og.T, dres, dctx)
 
 

time: 116 us -> 107 us (0.922)
  Pallas kernels: 115 us -> 107 us
    pallas_call x2, Pallas kernels: 115 us -> 107 us  [the longest x1 102 us: on_device(): pl.pallas_call(section_listed, out_shape=[VM(a.shape, a.dtype) for a in (...]
where the time goes in v3:
time: 107 us
  Pallas kernels  107 us (100%)
    pallas_call x1, Pallas kernels, on_device(): pl.pallas_call(section_listed, out_shape=[VM(a.shape, a.dtype) for a in (...  102 us
    pallas_call x1, Pallas kernels, on_device(): pl.pallas_call(hand_over_kernel, out_shape=[shape((4, 9, 128, 1024), BF16...  4.97 us

profile of v3, /device:TPU:1, one launch (start us, length us, event | category | flops | bytes accessed | tf_op | source)
XLA Modules:
  0.0 107.3 jit_solution(16730832821972969288)
XLA Ops:
  0.6 101.5 %section.1 = (bf16[9,4,128,1024]{3,2,1,0:T(8,128)(2,1)S(1)}, f32[1,1]{1,0:T(1,128)}, bf16[288,512]{1,0:T(8,128)(2,1)S(1)}, bf16[32,576]{1,0:T(8,128)(2,1)S(1)}, bf16[32,512]{1,0:T(8,128)(2,1)S(1)}) custom-call(bf16[32,512]{1,0:T(8,128)(2,1)} %refs_0_.1, bf16[32,576]{1,0:T(8,128)(2,1)} %refs_1_.1, bf16[288,512]{1,0:T(8,128)(2,1)} %bitcast.8, f32[4608]{0:T(1024)} %refs_3_.1, ...), custom_call_target="tpu_custom_call" | custom-call | flops 10000000000 | bytes 20000000 | tf_op jit(solution)/shard_map/section/pallas_call | solution.py:654
  102.2 5.0 %hand_over.1 = (bf16[4,9,128,1024]{3,2,1,0:T(8,128)(2,1)}, f32[1,1]{1,0:T(1,128)}, bf16[288,512]{1,0:T(8,128)(2,1)}, bf16[32,576]{1,0:T(8,128)(2,1)}, bf16[32,512]{1,0:T(8,128)(2,1)}) custom-call(bf16[9,4,128,1024]{3,2,1,0:T(8,128)(2,1)S(1)} %get-tuple-element.15.x_any, f32[1,1]{1,0:T(1,128)} %get-tuple-element.16.loss_in, ...), custom_call_target="tpu_custom_call" | custom-call | bytes 20000000 | tf_op jit(solution)/shard_map/hand_over/pallas_call | solution.py:674

commit v4 on v3

--- a/solution.py
+++ b/solution.py
@@ -13,6 +13,7 @@
 WIDTH = 4608
 SHARE = 1152
 PANELS = 9
+AHEAD = 2
 CHUNK = 8
 COLS = 288
 GATHER = (("y", "x", "z"), ("x", "z", "y"), ("z", "y", "x"))
@@ -46,11 +47,11 @@
     ctx_ref, res_ref, ow_ref, pg_ref, fg_ref, w_hbm, tgt_ref,
     x_out, loss_out, og_out, dres_out, dctx_out,
     wv, ctx, ow, pg, fg, rres, aout, ain, attn_s, stream_s, nbuf, gath, turned_q, cap, tgt, hot, part,
-    psrc, pipe_in, mp_in, scale, aim, grad,
-    keep, sib_out, sib_in, first, r1a, r1b, r1c, s2, own2, r2a, r2b, r2c, s3, r3,
+    psrc, pipe_in, mp_in, scale, aim, rise16, rises, falls, grad,
+    keep, sib_out, sib_in, first, r1a, r1b, r1c, s2, own2, r2a, r2b, r2c, s3, r3, rd,
     gsum, gout, gin, dcs, dcr, ogs, ogr, dsend, drecv,
-    w_sem, ctx_ss, ctx_rs, sib_ss, sib_rs, tn_ss, tn_rs, at_ss, at_rs, y_ss, y_rs, ag_ss, ag_rs, agc_ss, agc_rs, tp_ss, tp_rs, tm_ss, tm_rs,
-    rc_ss, rc_rs, rs_ss, rs_rs, ga_ss, ga_rs, dc_ss, dc_rs,
+    w_sem, ctx_ss, ctx_rs, sib_ss, sib_rs, tn_ss, tn_rs, at_ss, at_rs, y_ss, y_rs, ag_ss, ag_rs, agp_ss, agp_rs, agc_ss, agc_rs, tp_ss, tp_rs, tm_ss, tm_rs,
+    rc_ss, rc_rs, rs_ss, rs_rs, rsp_ss, rsp_rs, ga_ss, ga_rs, dc_ss, dc_rs,
 ):
     p, m = lax.axis_index("pipe"), lax.axis_index("mp")
     y, x, z, c = p // 4, p % 4, m // 2, m % 2
@@ -249,15 +250,29 @@
     def ag_wait(q, stage):
         landed(three_regions(q, stage), ag_rs.at[q, stage])
 
-    for q in range(PANELS):
+    def planes(j, dims):
+        return moved(moved(at, dims[0], j // 4), dims[1], j % 4)
+
+    def ag_plane(j, _):
+        for q in range(3):
+            src = region(q, at, ())
+            remote(src, src, agp_ss, agp_rs.at[q], place(planes(j, GATHER[q]))).start()
+        return 0
+
+    lax.fori_loop(1, 16, ag_plane, 0)
+    gone(turned_q.at[pl.ds(0, 3), pl.ds(0, 240), pl.ds(0, 128)], agp_ss)
+    for q in range(3, PANELS):
         ag_start(q, 0)
-    for q in range(PANELS):
+    for q in range(3, PANELS):
         ag_wait(q, 0)
         ag_start(q, 1)
 
     def ag_last(third):
         for q in range(third * 3, third * 3 + 3):
-            ag_wait(q, 1)
+            if third == 0:
+                landed(turned_q.at[q, pl.ds(0, 240), pl.ds(0, 128)], agp_rs.at[q])
+            else:
+                ag_wait(q, 1)
             ag_start(q, 2)
 
     def ag_sent(third):
@@ -300,7 +315,7 @@
             hot[rows, :] = hits
 
     for stage in range(2):
-        gone(three_regions(pl.ds(0, PANELS), stage), ag_ss.at[stage])
+        gone(three_regions(pl.ds(3, PANELS - 3), stage), ag_ss.at[stage])
 
     def ag_arrived(third):
         panels = pl.ds(third * 3, 3)
@@ -342,20 +357,6 @@
     lax.fori_loop(1, 16, pipe_send, 0)
     gone(pipe_in.at[pl.ds(0, 15)], tp_ss)
 
-    @pl.loop(0, PANELS)
-    def _(q):
-        turned_q[q] = gath[q].reshape(512, 512).T
-
-    landed(pipe_in.at[pl.ds(0, 15)], tp_rs)
-    mp_in[m] = jnp.sum(pipe_in[...], axis=0)
-
-    def mp_send(j, _):
-        remote(mp_in.at[m], mp_in.at[m], tm_ss, tm_rs, (p, lax.rem(m + j, 8))).start()
-        return 0
-
-    lax.fori_loop(1, 8, mp_send, 0)
-    gone(mp_in.at[pl.ds(0, 7)], tm_ss)
-
     @pl.loop(0, 16)
     def _(block):
         rows = rows_of(block * 32, 32)
@@ -366,9 +367,33 @@
             capped = cap[rows, cols]
             ratio = capped * (1.0 / softcap)
             slope = 1.0 - ratio * ratio
-            cap[rows, cols] = jnp.exp(capped) * slope
-            aim[rows, cols] = jnp.where(ids + j * 128 == wanted, slope, 0.0)
-
+            rise, fall = jnp.exp(capped) * slope, jnp.where(ids + j * 128 == wanted, slope, 0.0)
+            cap[rows, cols] = rise
+            aim[rows, cols] = fall
+            rise16[rows, cols] = rise.astype(BF16)
+            grad[rows, cols] = fall.astype(BF16)
+
+    def product_of(terms, q, which):
+        rows = rows_of(which * 256, 256)
+        return lax.dot_general(terms[rows, :], wv[q], (((1,), (1,)), ((), ())), preferred_element_type=F32)
+
+    def ahead(q):
+        for i, which in enumerate((1 - c, c)):
+            rises[q, i] = product_of(rise16, q, which)
+            falls[q, i] = product_of(grad, q, which)
+
+    ahead(0)
+    landed(pipe_in.at[pl.ds(0, 15)], tp_rs)
+    mp_in[m] = jnp.sum(pipe_in[...], axis=0)
+
+    def mp_send(j, _):
+        remote(mp_in.at[m], mp_in.at[m], tm_ss, tm_rs, (p, lax.rem(m + j, 8))).start()
+        return 0
+
+    lax.fori_loop(1, 8, mp_send, 0)
+    gone(mp_in.at[pl.ds(0, 7)], tm_ss)
+
+    ahead(1)
     landed(mp_in.at[pl.ds(0, 7)], tm_rs)
     sums = jnp.sum(mp_in[...], axis=0)
     totals, target_logit = sums[:4], sums[4:]
@@ -395,7 +420,7 @@
         )
 
     def rs_sib(q):
-        sib_out[q] = grad_dot(q, 1 - c).astype(BF16)
+        sib_out[q] = (grad_dot(q, 1 - c) if q >= AHEAD else joined(q, 0, 1 - c)).astype(BF16)
         remote(sib_out.at[q], sib_in.at[q], rc_ss, rc_rs.at[q], sib).start()
 
     def piece(ref, dim, index, left, lead):
@@ -423,6 +448,11 @@
             src = first.at[piece(first, dim, there[dim], ("z", "x", "y"), (q,))]
             remote(src, r1[q % 3].at[q // 3, by - 1], rs_ss.at[q % 3, 0], rs_rs.at[q, 0], place(there)).start()
 
+    def rs_block(k, there):
+        where = [d for d in ("z", "x") if d != dims_of(k)[0]]
+        cols = pl.ds(0, 128) if k == 1 else lanes(there["y"] * 128, 128)
+        return (2, *(there[d] for d in where), pl.ds(0, 16), cols)
+
     def rs_second(q):
         k, r = q % 3, q // 3
         got = r1[k].at[r]
@@ -434,6 +464,16 @@
         total = total + got[0].astype(F32) + got[1].astype(F32) + got[2].astype(F32)
         own2[k][r] = total
         s2[k][r] = total.astype(BF16)
+        if r == 2:
+            def rs_plane(j, _):
+                there = planes(j, dims[1:])
+                remote(
+                    s2[k].at[rs_block(k, there)], rd.at[k, j], rsp_ss, rsp_rs.at[k], place(there)
+                ).start()
+                return 0
+
+            lax.fori_loop(1, 16, rs_plane, 0)
+            return
         for by in NEAR:
             there = moved(at, dims[1], by)
             src = s2[k].at[piece(s2[k], dims[1], there[dims[1]], left, (r,))]
@@ -463,31 +503,51 @@
     def head_early(q):
         x_out[q] = jnp.dot(turned_q[q], grad[...], preferred_element_type=F32).astype(BF16).reshape(4, 128, 1024)
 
+    def joined(q, i, which):
+        inv = scale[rows_of(which * 256, 256), :]
+        return jnp.concatenate(
+            [rises[q, i, :, n : n + 128] * inv - falls[q, i, :, n : n + 128] for n in range(0, 512, 128)], axis=1
+        ).reshape(4, 4, 16, 512)
+
+    rs_sib(0)
+    rs_sib(1)
+    keep[0] = joined(0, 1, c)
+    keep[1] = joined(1, 1, c)
     logit_grad(1 - c)
-    rs_sib(0)
     logit_grad(c)
-    rs_sib(1)
     for q in range(PANELS):
-        keep[q] = grad_dot(q, c)
+        if q >= AHEAD:
+            keep[q] = grad_dot(q, c)
         if q + 2 < PANELS:
             rs_sib(q + 2)
         rs_first(q)
+    @pl.loop(0, PANELS)
+    def _(q):
+        turned_q[q] = gath[q].reshape(512, 512).T
+
     head_early(0)
     for q in range(PANELS):
         rs_second(q)
     for q in (1, 2, 3):
         head_early(q)
-    for q in range(PANELS):
+    for q in range(PANELS - 3):
         rs_third(q)
     for q in (4, 5):
         head_early(q)
-    for q in range(PANELS):
+    for q in range(PANELS - 3):
         rs_last(q)
+    gone(rd.at[:, pl.ds(1, 15)], rsp_ss)
+    for k in range(3):
+        landed(rd.at[k, pl.ds(1, 15)], rsp_rs.at[k])
+        total = own2[k][rs_block(k, at)]
+        for j in range(1, 16):
+            total = total + rd[k, j].astype(F32)
+        gsum[:, (k + 6) * 128 : (k + 7) * 128] = total
     gone(sib_out, rc_ss)
     for k in range(3):
         gone(r1[k], rs_ss.at[k, 0])
-        gone(r2[k], rs_ss.at[k, 1])
-        gone(r3.at[pl.ds(0, 3)], rs_ss.at[k, 2])
+        gone(r2[k].at[pl.ds(0, 2)], rs_ss.at[k, 1])
+        gone(r3.at[pl.ds(0, 2)], rs_ss.at[k, 2])
 
     stream, attn = stream_s[...], attn_s[...]
     inv_attn, inv_stream = nbuf[2, 0][:, :1], nbuf[2, 1][:, :1]
@@ -592,6 +652,9 @@
     VM((512, 128), F32),
     VM((512, 1024), F32),
     VM((512, 1024), BF16),
+    VM((AHEAD, 2, 256, 512), F32),
+    VM((AHEAD, 2, 256, 512), F32),
+    VM((512, 1024), BF16),
     VM((9, 4, 4, 16, 512), F32),
     VM((9, 4, 4, 16, 512), BF16),
     VM((9, 4, 4, 16, 512), BF16),
@@ -606,6 +669,7 @@
     VM((3, 3, 4, 16, 128), BF16),
     (VM((3, 16, 512), F32), VM((3, 4, 16, 128), F32), VM((3, 4, 16, 128), F32)),
     VM((9, 3, 16, 128), F32),
+    VM((3, 16, 16, 128), BF16),
     VM((16, SHARE), F32),
     VM((4, 16, COLS), BF16),
     VM((16, 16, COLS), BF16),
@@ -623,10 +687,12 @@
     DMA((2,)), DMA((2,)),
     DMA((5,)), DMA((9, 3)),
     DMA, DMA((3,)),
+    DMA, DMA((3,)),
     DMA, DMA,
     DMA, DMA,
     DMA, DMA((9,)),
     DMA((3, 3)), DMA((9, 3)),
+    DMA, DMA((3,)),
     DMA, DMA,
     DMA, DMA,
 ]
@@ -658,7 +724,7 @@
         out_specs=[vmem, vmem, vmem, vmem, vmem],
         scratch_shapes=FLAT,
         compiler_params=pltpu.CompilerParams(
-            collective_id=0, has_side_effects=True, vmem_limit_bytes=46 * 2**20
+            collective_id=0, has_side_effects=True, vmem_limit_bytes=52 * 2**20
         ),
         cost_estimate=pl.CostEstimate(flops=10**10, bytes_accessed=20 * 10**6, transcendentals=10**6),
         name="section",

time: 107 us -> 104 us (0.972)
  Pallas kernels: 107 us -> 104 us
    pallas_call x1, Pallas kernels: 102 us -> 98.6 us  [on_device(): pl.pallas_call(section_listed, out_shape=[VM(a.shape, a.dtype) for a in (...]
where the time goes in v4:
time: 104 us
  Pallas kernels  104 us (100%)
    pallas_call x1, Pallas kernels, on_device(): pl.pallas_call(section_listed, out_shape=[VM(a.shape, a.dtype) for a in (...  98.6 us
    pallas_call x1, Pallas kernels, on_device(): pl.pallas_call(hand_over_kernel, out_shape=[shape((4, 9, 128, 1024), BF16...  4.97 us

profile of v4, /device:TPU:1, one launch (start us, length us, event | category | flops | bytes accessed | tf_op | source)
XLA Modules:
  0.0 104.3 jit_solution(16077082835065339591)
XLA Ops:
  0.6 98.6 %section.1 = (bf16[9,4,128,1024]{3,2,1,0:T(8,128)(2,1)S(1)}, f32[1,1]{1,0:T(1,128)}, bf16[288,512]{1,0:T(8,128)(2,1)S(1)}, bf16[32,576]{1,0:T(8,128)(2,1)S(1)}, bf16[32,512]{1,0:T(8,128)(2,1)S(1)}) custom-call(bf16[32,512]{1,0:T(8,128)(2,1)} %refs_0_.1, bf16[32,576]{1,0:T(8,128)(2,1)} %refs_1_.1, bf16[288,512]{1,0:T(8,128)(2,1)} %bitcast.8, f32[4608]{0:T(1024)} %refs_3_.1, ...), custom_call_target="tpu_custom_call" | custom-call | flops 10000000000 | bytes 20000000 | tf_op jit(solution)/shard_map/section/pallas_call | solution.py:720
  99.2 5.0 %hand_over.1 = (bf16[4,9,128,1024]{3,2,1,0:T(8,128)(2,1)}, f32[1,1]{1,0:T(1,128)}, bf16[288,512]{1,0:T(8,128)(2,1)}, bf16[32,576]{1,0:T(8,128)(2,1)}, bf16[32,512]{1,0:T(8,128)(2,1)}) custom-call(bf16[9,4,128,1024]{3,2,1,0:T(8,128)(2,1)S(1)} %get-tuple-element.15.x_any, f32[1,1]{1,0:T(1,128)} %get-tuple-element.16.loss_in, ...), custom_call_target="tpu_custom_call" | custom-call | bytes 20000000 | tf_op jit(solution)/shard_map/hand_over/pallas_call | solution.py:740

commit v5 on v4

--- a/solution.py
+++ b/solution.py
@@ -14,7 +14,7 @@
 SHARE = 1152
 PANELS = 9
 AHEAD = 2
-CHUNK = 8
+CHUNK = 4
 COLS = 288
 GATHER = (("y", "x", "z"), ("x", "z", "y"), ("z", "y", "x"))
 NEAR = (1, 3, 2)

time: 104 us -> 104 us (level)
  no operation moved by 1% of the time
where the time goes in v5:
time: 104 us; the launch traced here: 103 us
  Pallas kernels  103 us (99%)
    pallas_call x1, Pallas kernels, on_device(): pl.pallas_call(section_listed, out_shape=[VM(a.shape, a.dtype) for a in (...  97.7 us
    pallas_call x1, Pallas kernels, on_device(): pl.pallas_call(hand_over_kernel, out_shape=[shape((4, 9, 128, 1024), BF16...  4.97 us

profile of v5, /device:TPU:1, one launch (start us, length us, event | category | flops | bytes accessed | tf_op | source)
XLA Modules:
  0.0 103.4 jit_solution(15516530794158949691)
XLA Ops:
  0.6 97.7 %section.1 = (bf16[9,4,128,1024]{3,2,1,0:T(8,128)(2,1)S(1)}, f32[1,1]{1,0:T(1,128)}, bf16[288,512]{1,0:T(8,128)(2,1)S(1)}, bf16[32,576]{1,0:T(8,128)(2,1)S(1)}, bf16[32,512]{1,0:T(8,128)(2,1)S(1)}) custom-call(bf16[32,512]{1,0:T(8,128)(2,1)} %refs_0_.1, bf16[32,576]{1,0:T(8,128)(2,1)} %refs_1_.1, bf16[288,512]{1,0:T(8,128)(2,1)} %bitcast.8, f32[4608]{0:T(1024)} %refs_3_.1, ...), custom_call_target="tpu_custom_call" | custom-call | flops 10000000000 | bytes 20000000 | tf_op jit(solution)/shard_map/section/pallas_call | solution.py:720
  98.3 5.0 %hand_over.1 = (bf16[4,9,128,1024]{3,2,1,0:T(8,128)(2,1)}, f32[1,1]{1,0:T(1,128)}, bf16[288,512]{1,0:T(8,128)(2,1)}, bf16[32,576]{1,0:T(8,128)(2,1)}, bf16[32,512]{1,0:T(8,128)(2,1)}) custom-call(bf16[9,4,128,1024]{3,2,1,0:T(8,128)(2,1)S(1)} %get-tuple-element.15.x_any, f32[1,1]{1,0:T(1,128)} %get-tuple-element.16.loss_in, ...), custom_call_target="tpu_custom_call" | custom-call | bytes 20000000 | tf_op jit(solution)/shard_map/hand_over/pallas_call | solution.py:740
